TPU v7x, 32 devices: a whole 2x2x4 slice. The times are simulated.
32 devices in a mesh: lat: 4 (over z), lon: 8 (over y, x, core).
Axes of the slice: x: 2, y: 2, z: 4, core: 2. Of those that a mesh axis runs over, the one named last changes fastest.
Arguments:
- features: bfloat16 [16384, 64], P(('lat', 'lon')), may hold values from -6 to 6
- land_tile: int32 [16384, 1], P(('lat', 'lon')), may hold values from 0 to 31; in each aligned block of 512 rows (0 to 511, 512 to 1023, ...) at most 32 rows name the same one
- land_spot: int32 [16384], P(('lat', 'lon')), may hold values from 0 to 1023
- w_in: bfloat16 [64, 256], replicated, may hold values from -0.75 to 0.75
- b_in: float32 [256], replicated, may hold values from -3 to 3
- w_mid: bfloat16 [256, 256], replicated, may hold values from -0.375 to 0.375
- b_mid: float32 [256], replicated, may hold values from -3 to 3
- w_out: bfloat16 [256, 16], replicated, may hold values from -0.375 to 0.375
- tracers: float32 [16, 16, 32, 1024], P(None, None, 'lat', 'lon'), may hold values from -6 to 6
- zonal_wind: float32 [16, 32, 1024], P(None, 'lat', 'lon'), may hold values from -0.95 to 0.95
- meridional_wind: float32 [16, 32, 1024], P(None, 'lat', 'lon'), may hold values from -0.95 to 0.95
- mixing: float32 [32, 16, 16], P('lat'), may hold values from 0 to 0.8, as said below
Outputs:
- tracers_out: float32 [16, 16, 32, 1024], P(None, None, 'lat', 'lon')
Inputs may be any that keep to these rules, and one draw needn't show every extreme that they name: `land_tile`: in each aligned block of 512 rows (the land cells of one device), no tile is named by more than 32 rows, a bound that some block reaches; every tile is named somewhere. `mixing`: entries are nonnegative.
All inputs are finite; a program needn't handle non-finite values.
Results may differ from a plain program's by a relative error of at most 0.00044.
Values sent between devices are 32-bit elements; how exact they have to be, the bound alone decides.
A program may use at most 64 MiB of HBM per device.

v0:
```python
import jax
import jax.numpy as jnp
from jax import lax
from jax.sharding import PartitionSpec as P

SUBSTEPS = 2


def with_halo(block, sides, width, periodic):
    for axis, dim in sides:
        count = lax.axis_size(axis)
        forward = [(i, i + 1) for i in range(count - 1)]
        if periodic:
            forward.append((count - 1, 0))
        backward = [(target, source) for source, target in forward]
        low = lax.ppermute(
            lax.slice_in_dim(block, block.shape[dim] - width, None, axis=dim), axis, forward
        )
        high = lax.ppermute(lax.slice_in_dim(block, 0, width, axis=dim), axis, backward)
        block = jnp.concatenate([low, block, high], axis=dim)
    return block


def section(values, start, stop, axis):
    return lax.slice_in_dim(values, start, values.shape[axis] + stop, axis=axis)


def transport(values, courant, axis):
    edges = 7.0 / 12.0 * (
        section(values, 1, -2, axis) + section(values, 2, -1, axis)
    ) - 1.0 / 12.0 * (section(values, 0, -3, axis) + section(values, 3, 0, axis))
    left_edge = section(edges, 0, -1, axis)
    right_edge = section(edges, 1, 0, axis)
    centre = section(values, 2, -2, axis)
    slope = right_edge - left_edge
    curve = 6.0 * (centre - 0.5 * (left_edge + right_edge))
    face_courant = section(courant, 2, -3, axis)
    upwind = face_courant * (
        section(right_edge, 0, -1, axis)
        - 0.5
        * face_courant
        * (
            section(slope, 0, -1, axis)
            - (1.0 - 2.0 / 3.0 * face_courant) * section(curve, 0, -1, axis)
        )
    )
    reverse = -face_courant
    backward = face_courant * (
        section(left_edge, 1, 0, axis)
        + 0.5
        * reverse
        * (section(slope, 1, 0, axis) + (1.0 - 2.0 / 3.0 * reverse) * section(curve, 1, 0, axis))
    )
    crossing = jnp.where(face_courant >= 0, upwind, backward)
    return section(values, 3, -3, axis) - (
        section(crossing, 1, 0, axis) - section(crossing, 0, -1, axis)
    )


def on_device(
    features,
    land_tile,
    land_spot,
    w_in,
    b_in,
    w_mid,
    b_mid,
    w_out,
    tracers,
    zonal_wind,
    meridional_wind,
    mixing,
):
    first = jax.nn.silu(jnp.dot(features, w_in, preferred_element_type=jnp.float32) + b_in).astype(
        jnp.bfloat16
    )
    second = jax.nn.silu(jnp.dot(first, w_mid, preferred_element_type=jnp.float32) + b_mid).astype(
        jnp.bfloat16
    )
    surface_flux = jnp.dot(second, w_out, preferred_element_type=jnp.float32)
    tracer_count = surface_flux.shape[1]
    lat_count = lax.axis_size("lat")
    lon_count = lax.axis_size("lon")
    device_count = lat_count * lon_count
    capacity = 2 * surface_flux.shape[0] // device_count
    owner_tile = land_tile[:, 0]
    member = (owner_tile[:, None] == jnp.arange(device_count, dtype=jnp.int32)[None, :]).astype(
        jnp.int32
    )
    earlier = jnp.cumsum(member, axis=0) - member
    slot_index = jnp.sum(earlier * member, axis=1)
    outgoing = (
        jnp.zeros((device_count, capacity, tracer_count), jnp.float32)
        .at[owner_tile, slot_index]
        .set(surface_flux)
    )
    places = (
        jnp.zeros((device_count, capacity), jnp.float32)
        .at[owner_tile, slot_index]
        .set(land_spot.astype(jnp.float32))
    )
    arrived_flux, arrived_places = (
        lax.all_to_all(outgoing, ("lat", "lon"), split_axis=0, concat_axis=0, tiled=True),
        lax.all_to_all(places, ("lat", "lon"), split_axis=0, concat_axis=0, tiled=True),
    )
    _, levels, tile_rows, tile_cols = tracers.shape
    positions = arrived_places.reshape(-1).astype(jnp.int32)
    emitted = (
        jnp.zeros((tile_rows * tile_cols, tracer_count), jnp.float32)
        .at[positions]
        .add(arrived_flux.reshape(-1, tracer_count))
    )
    state = tracers.at[:, 0].add(emitted.T.reshape(tracer_count, tile_rows, tile_cols))
    global_rows = lax.axis_index("lat") * tile_rows + jnp.arange(tile_rows, dtype=jnp.int32)
    northern = (global_rows < tile_rows * lat_count - 1).astype(jnp.float32)
    meridional = (meridional_wind * northern[None, :, None])[None]
    zonal = zonal_wind[None]
    for substep in range(SUBSTEPS):
        joined = jnp.concatenate([state, zonal], axis=0)
        widened = with_halo(joined, (("lon", 3),), 3, True)
        state = transport(widened[:-1], widened[-1:], 3)
    for substep in range(SUBSTEPS):
        joined = jnp.concatenate([state, meridional], axis=0)
        widened = with_halo(joined, (("lat", 2),), 3, False)
        state = transport(widened[:-1], widened[-1:], 2)
    return jnp.einsum("akj,tjab->tkab", mixing, state, precision=lax.Precision.HIGHEST)


def solution(mesh):
    placed = (
        P(("lat", "lon"), None),
        P(("lat", "lon"), None),
        P(("lat", "lon")),
        P(),
        P(),
        P(),
        P(),
        P(),
        P(None, None, "lat", "lon"),
        P(None, "lat", "lon"),
        P(None, "lat", "lon"),
        P("lat", None, None),
    )
    return jax.shard_map(
        on_device,
        mesh=mesh,
        in_specs=placed,
        out_specs=P(None, None, "lat", "lon"),
        check_vma=False,
    )
```

profile of v0, /device:TPU:0, one launch (start us, length us, event | category | flops | bytes accessed | tf_op | source)
XLA Modules:
  0.0 203.0 jit_solution(13258684636253238236)
XLA Ops:
  0.0 0.7 convert_element_type.38
  0.7 0.7 fusion.88
  1.4 1.2 reduce-window.6
  2.8 0.8 fusion.86
  3.6 0.7 or_select_fusion
  4.9 66.6 %scatter_fusion = f32[32,32]{1,0:T(8,128)} fusion(f32[32,32]{1,0:T(8,128)} %broadcast_in_dim.59, s32[512]{0:T(512)S(1)} %bitcast.99, f32[512]{0:T(512)S(1)} %convert_element_type.38), kind=kCustom, calls=%fused_computation | custom fusion | bytes 10240 | tf_op jit(solution)/shard_map/scatter | solution.py:100
  71.5 7.9 %all-to-all-start = ((f32[32,1,32]{2,1,0:T(1,128)}), f32[32,1,32]{2,1,0:T(1,128)S(1)}, u32[]{:S(2)}, u32[]{:S(2)}) async-start(f32[32,1,32]{2,1,0:T(1,128)} %bitcast.7), calls=%async_computation | async-start | bytes 32768 | tf_op jit(solution)/shard_map/all_to_all | solution.py:104
  80.2 0.8 copy-done.6
  81.3 24.2 %scatter_fusion.1 = f32[32,32,16]{2,1,0:T(8,128)S(1)} fusion(f32[32,32,16]{2,1,0:T(8,128)S(1)} %broadcast_in_dim.60, s32[512]{0:T(512)S(1)} %bitcast.100, f32[512,16]{1,0:T(8,128)S(1)} %fusion.77), kind=kCustom, calls=%fused_computation.1 | custom fusion | bytes 102400 | tf_op jit(solution)/shard_map/scatter | solution.py:95
  105.8 0.8 reshape.137
  106.6 5.8 %all-to-all-start.1 = ((f32[32,1,512]{2,1,0:T(1,128)}), f32[32,1,512]{2,1,0:T(1,128)S(1)}, u32[]{:S(2)}, u32[]{:S(2)}) async-start(f32[32,1,512]{2,1,0:T(1,128)} %reshape.137), calls=%async_computation.1 | async-start | bytes 131072 | tf_op jit(solution)/shard_map/all_to_all | solution.py:103
  112.5 7.3 %all-to-all-done.1 = f32[32,1,512]{2,1,0:T(1,128)S(1)} async-done(((f32[32,1,512]{2,1,0:T(1,128)}), f32[32,1,512]{2,1,0:T(1,128)S(1)}, u32[]{:S(2)}, u32[]{:S(2)}) %all-to-all-start.1) | async-done | bytes 65568 | tf_op jit(solution)/shard_map/all_to_all | solution.py:103
  120.3 0.8 reduce.8
  121.5 6.7 %scatter_custom_fusion.2 = f32[1024,16]{1,0:T(8,128)S(1)} fusion(s32[1024]{0:T(1024)S(1)} %bitcast.110, f32[1024,16]{1,0:T(8,128)S(1)} %bitcast.105, f32[]{:T(128)} %constant.63.clone.1), kind=kCustom, calls=%fused_computation.136 | custom fusion | flops 16384 | bytes 65540 | tf_op jit(solution)/shard_map/scatter-add | solution.py:111
  128.4 1.3 scatter-add.13
  130.1 1.7 copy.110
  131.8 1.0 copy.116
  132.8 2.9 %collective-permute-start.1 = (f32[17,16,8,3]{0,2,3,1:T(8,128)S(1)}, f32[17,16,8,3]{0,2,3,1:T(8,128)}, u32[]{:S(2)}, u32[]{:S(2)}) collective-permute-start(f32[17,16,8,3]{0,2,3,1:T(8,128)S(1)} %copy.116), channel_id=1, source_target_pairs={{1,0},{2,1},{3,2},{4,3},{5,4},{6,5},{7,6},{0,7},{9,8},{10,9},{11,1... | collective-permute-start | bytes 78344 | tf_op jit(solution)/shard_map/ppermute | solution.py:19
  135.6 3.7 %collective-permute-done = f32[17,16,8,3]{0,2,3,1:T(8,128)S(1)} collective-permute-done((f32[17,16,8,3]{0,2,3,1:T(8,128)}, f32[17,16,8,3]{0,2,3,1:T(8,128)S(1)}, u32[]{:S(2)}, u32[]{:S(2)}) %collective-permute-start) | collective-permute-done | bytes 26144 | tf_op jit(solution)/shard_map/ppermute | solution.py:16
  139.3 1.3 copy.111
  141.3 1.1 slice_bitcast_fusion.1
  142.8 2.2 %copy.118 = f32[17,16,8,3]{3,1,2,0:T(8,128)S(1)} copy(f32[17,16,8,3]{0,2,3,1:T(8,128)} %collective-permute-done.1) | data formatting | bytes 52224 | tf_op jit(solution)/shard_map/ppermute | solution.py:19
  145.1 0.9 fusion.1
  146.0 0.7 copy-done.5
  146.7 1.2 fusion.9
  147.9 1.2 slice_subtract_fusion.3
  149.2 1.7 fusion.29
  151.6 1.7 copy.129
  153.4 1.0 copy.135
  154.3 2.9 %collective-permute-start.3 = (f32[17,16,8,3]{0,2,3,1:T(8,128)S(1)}, f32[17,16,8,3]{0,2,3,1:T(8,128)}, u32[]{:S(2)}, u32[]{:S(2)}) collective-permute-start(f32[17,16,8,3]{0,2,3,1:T(8,128)S(1)} %copy.135), channel_id=1, source_target_pairs={{1,0},{2,1},{3,2},{4,3},{5,4},{6,5},{7,6},{0,7},{9,8},{10,9},{11,1... | collective-permute-start | bytes 78344 | tf_op jit(solution)/shard_map/ppermute | solution.py:19
  157.2 3.0 %collective-permute-done.2 = f32[17,16,8,3]{0,2,3,1:T(8,128)S(1)} collective-permute-done((f32[17,16,8,3]{0,2,3,1:T(8,128)}, f32[17,16,8,3]{0,2,3,1:T(8,128)S(1)}, u32[]{:S(2)}, u32[]{:S(2)}) %collective-permute-start.2) | collective-permute-done | bytes 26144 | tf_op jit(solution)/shard_map/ppermute | solution.py:16
  160.2 1.2 copy.130
  162.2 1.1 slice_bitcast_fusion
  163.7 2.2 %copy.137 = f32[17,16,8,3]{3,1,2,0:T(8,128)S(1)} copy(f32[17,16,8,3]{0,2,3,1:T(8,128)} %collective-permute-done.3) | data formatting | bytes 52224 | tf_op jit(solution)/shard_map/ppermute | solution.py:19
  165.9 0.9 fusion.3
  167.6 1.2 fusion.13
  168.8 1.2 slice_subtract_fusion.2
  170.1 1.7 fusion.18
  172.2 2.7 %collective-permute-start.4 = (f32[17,16,3,128]{3,1,2,0:T(8,128)S(1)}, f32[17,16,3,128]{3,1,2,0:T(8,128)S(1)}, u32[]{:S(2)}, u32[]{:S(2)}) collective-permute-start(f32[17,16,3,128]{3,1,2,0:T(8,128)S(1)} %get-tuple-element.47), channel_id=1, source_target_pairs={{0,8},{8,16},{16,24},{1,9},{9,17},{17,25},{2,10},{10,18},{18,26},{... | collective-permute-start | bytes 1253384 | tf_op jit(solution)/shard_map/ppermute | solution.py:16
  174.9 1.3 collective-permute-start.5
  176.2 4.2 %collective-permute-done.4 = f32[17,16,3,128]{3,1,2,0:T(8,128)S(1)} collective-permute-done((f32[17,16,3,128]{3,1,2,0:T(8,128)S(1)}, f32[17,16,3,128]{3,1,2,0:T(8,128)S(1)}, u32[]{:S(2)}, u32[]{:S(2)}) %collective-permute-start.4) | collective-permute-done | bytes 417824 | tf_op jit(solution)/shard_map/ppermute | solution.py:16
  180.6 4.2 %collective-permute-done.5 = f32[17,16,3,128]{3,1,2,0:T(8,128)S(1)} collective-permute-done((f32[17,16,3,128]{3,1,2,0:T(8,128)S(1)}, f32[17,16,3,128]{3,1,2,0:T(8,128)S(1)}, u32[]{:S(2)}, u32[]{:S(2)}) %collective-permute-start.5) | collective-permute-done | bytes 417824 | tf_op jit(solution)/shard_map/ppermute | solution.py:19
  186.3 2.4 %collective-permute-start.6 = (f32[17,16,3,128]{3,1,2,0:T(8,128)S(1)}, f32[17,16,3,128]{3,1,2,0:T(8,128)S(1)}, u32[]{:S(2)}, u32[]{:S(2)}) collective-permute-start(f32[17,16,3,128]{3,1,2,0:T(8,128)S(1)} %get-tuple-element.45), channel_id=1, source_target_pairs={{0,8},{8,16},{16,24},{1,9},{9,17},{17,25},{2,10},{10,18},{18,26},{... | collective-permute-start | bytes 1253384 | tf_op jit(solution)/shard_map/ppermute | solution.py:16
  188.8 1.6 collective-permute-start.7
  190.3 4.0 %collective-permute-done.6 = f32[17,16,3,128]{3,1,2,0:T(8,128)S(1)} collective-permute-done((f32[17,16,3,128]{3,1,2,0:T(8,128)S(1)}, f32[17,16,3,128]{3,1,2,0:T(8,128)S(1)}, u32[]{:S(2)}, u32[]{:S(2)}) %collective-permute-start.6) | collective-permute-done | bytes 417824 | tf_op jit(solution)/shard_map/ppermute | solution.py:16
  194.5 4.2 %collective-permute-done.7 = f32[17,16,3,128]{3,1,2,0:T(8,128)S(1)} collective-permute-done((f32[17,16,3,128]{3,1,2,0:T(8,128)S(1)}, f32[17,16,3,128]{3,1,2,0:T(8,128)S(1)}, u32[]{:S(2)}, u32[]{:S(2)}) %collective-permute-start.7) | collective-permute-done | bytes 417824 | tf_op jit(solution)/shard_map/ppermute | solution.py:19
  200.3 1.1 convolution_bitcast_fusion
  201.4 1.6 copy.150
  (99 shorter events, 11.3 us)
Async XLA Ops:
  0.0 79.8 %copy-start = (bf16[256,256]{1,0:T(8,128)(2,1)S(1)}, bf16[256,256]{1,0:T(8,128)(2,1)}, u32[]{:S(2)}) copy-start(bf16[256,256]{1,0:T(8,128)(2,1)} %param.19) | copy-start | bytes 393220
  4.9 74.5 %copy-start.19 = (bf16[512,64]{0,1:T(8,128)(2,1)S(1)}, bf16[512,64]{0,1:T(8,128)(2,1)}, u32[]{:S(2)}) copy-start(bf16[512,64]{0,1:T(8,128)(2,1)} %param.14) | copy-start | bytes 196612
  4.9 74.5 %copy-start.20 = (bf16[64,256]{1,0:T(8,128)(2,1)S(1)}, bf16[64,256]{1,0:T(8,128)(2,1)}, u32[]{:S(2)}) copy-start(bf16[64,256]{1,0:T(8,128)(2,1)} %param.17) | copy-start | bytes 98308
  4.9 74.5 %copy-start.22 = (f32[256]{0:T(256)S(1)}, f32[256]{0:T(256)}, u32[]{:S(2)}) copy-start(f32[256]{0:T(256)} %param.18) | copy-start | bytes 3076
  71.5 8.3 %copy-start.21 = (bf16[256,16]{0,1:T(8,128)(2,1)S(1)}, bf16[256,16]{0,1:T(8,128)(2,1)}, u32[]{:S(2)}) copy-start(bf16[256,16]{0,1:T(8,128)(2,1)} %param.21) | copy-start | bytes 24580
  71.5 8.3 %copy-start.23 = (f32[256]{0:T(256)S(1)}, f32[256]{0:T(256)}, u32[]{:S(2)}) copy-start(f32[256]{0:T(256)} %param.20) | copy-start | bytes 3076
  71.5 35.0 %all-to-all-start = ((f32[32,1,32]{2,1,0:T(1,128)}), f32[32,1,32]{2,1,0:T(1,128)S(1)}, u32[]{:S(2)}, u32[]{:S(2)}) async-start(f32[32,1,32]{2,1,0:T(1,128)} %bitcast.7), calls=%async_computation | async-start | bytes 32768 | tf_op jit(solution)/shard_map/all_to_all | solution.py:104
  79.8 1.2 copy-start.6
  79.8 1.4 copy-start.17
  105.5 22.8 %slice-start = ((f32[16,16,8,128]{3,2,1,0:T(8,128)}), f32[16,1,8,128]{3,2,1,0:T(8,128)S(1)}, s32[]{:S(2)}) async-start(f32[16,16,8,128]{3,2,1,0:T(8,128)} %param.22), calls=%async_computation.2 | async-start | bytes 131072 | tf_op jit(solution)/shard_map/slice.78
  106.6 13.2 %all-to-all-start.1 = ((f32[32,1,512]{2,1,0:T(1,128)}), f32[32,1,512]{2,1,0:T(1,128)S(1)}, u32[]{:S(2)}, u32[]{:S(2)}) async-start(f32[32,1,512]{2,1,0:T(1,128)} %reshape.137), calls=%async_computation.1 | async-start | bytes 131072 | tf_op jit(solution)/shard_map/all_to_all | solution.py:103
  131.8 7.6 %collective-permute-start = (f32[17,16,8,3]{0,2,3,1:T(8,128)}, f32[17,16,8,3]{0,2,3,1:T(8,128)S(1)}, u32[]{:S(2)}, u32[]{:S(2)}) collective-permute-start(f32[17,16,8,3]{0,2,3,1:T(8,128)} %copy.110), channel_id=1, source_target_pairs={{0,1},{1,2},{2,3},{3,4},{4,5},{5,6},{6,7},{7,0},{8,9},{9,10},{10,1... | collective-permute-start | bytes 78344 | tf_op jit(solution)/shard_map/ppermute | solution.py:16
  132.8 10.0 %collective-permute-start.1 = (f32[17,16,8,3]{0,2,3,1:T(8,128)S(1)}, f32[17,16,8,3]{0,2,3,1:T(8,128)}, u32[]{:S(2)}, u32[]{:S(2)}) collective-permute-start(f32[17,16,8,3]{0,2,3,1:T(8,128)S(1)} %copy.116), channel_id=1, source_target_pairs={{1,0},{2,1},{3,2},{4,3},{5,4},{6,5},{7,6},{0,7},{9,8},{10,9},{11,1... | collective-permute-start | bytes 78344 | tf_op jit(solution)/shard_map/ppermute | solution.py:19
  141.3 1.5 copy-start.4
  145.0 1.6 copy-start.5
  147.9 1.2 copy-start.12
  147.9 1.2 copy-start.13
  147.9 1.2 copy-start.14
  147.9 1.2 copy-start.15
  151.2 2.1 %copy-start.18 = (f32[16,8,128]{2,1,0:T(8,128)S(1)}, f32[16,8,128]{2,1,0:T(8,128)}, u32[]{:S(2)}) copy-start(f32[16,8,128]{2,1,0:T(8,128)} %param.24) | copy-start | bytes 196612
  153.3 7.0 %collective-permute-start.2 = (f32[17,16,8,3]{0,2,3,1:T(8,128)}, f32[17,16,8,3]{0,2,3,1:T(8,128)S(1)}, u32[]{:S(2)}, u32[]{:S(2)}) collective-permute-start(f32[17,16,8,3]{0,2,3,1:T(8,128)} %copy.129), channel_id=1, source_target_pairs={{0,1},{1,2},{2,3},{3,4},{4,5},{5,6},{6,7},{7,0},{8,9},{9,10},{10,1... | collective-permute-start | bytes 78344 | tf_op jit(solution)/shard_map/ppermute | solution.py:16
  154.3 9.4 %collective-permute-start.3 = (f32[17,16,8,3]{0,2,3,1:T(8,128)S(1)}, f32[17,16,8,3]{0,2,3,1:T(8,128)}, u32[]{:S(2)}, u32[]{:S(2)}) collective-permute-start(f32[17,16,8,3]{0,2,3,1:T(8,128)S(1)} %copy.135), channel_id=1, source_target_pairs={{1,0},{2,1},{3,2},{4,3},{5,4},{6,5},{7,6},{0,7},{9,8},{10,9},{11,1... | collective-permute-start | bytes 78344 | tf_op jit(solution)/shard_map/ppermute | solution.py:19
  162.1 1.6 copy-start.2
  165.9 1.6 copy-start.3
  168.8 1.2 copy-start.7
  168.8 1.2 copy-start.8
  168.8 1.2 copy-start.9
  168.8 1.2 copy-start.10
  168.8 1.2 copy-start.11
  172.2 8.2 %collective-permute-start.4 = (f32[17,16,3,128]{3,1,2,0:T(8,128)S(1)}, f32[17,16,3,128]{3,1,2,0:T(8,128)S(1)}, u32[]{:S(2)}, u32[]{:S(2)}) collective-permute-start(f32[17,16,3,128]{3,1,2,0:T(8,128)S(1)} %get-tuple-element.47), channel_id=1, source_target_pairs={{0,8},{8,16},{16,24},{1,9},{9,17},{17,25},{2,10},{10,18},{18,26},{... | collective-permute-start | bytes 1253384 | tf_op jit(solution)/shard_map/ppermute | solution.py:16
  174.9 9.9 %collective-permute-start.5 = (f32[17,16,3,128]{3,1,2,0:T(8,128)S(1)}, f32[17,16,3,128]{3,1,2,0:T(8,128)S(1)}, u32[]{:S(2)}, u32[]{:S(2)}) collective-permute-start(f32[17,16,3,128]{3,1,2,0:T(8,128)S(1)} %get-tuple-element.48), channel_id=1, source_target_pairs={{8,0},{16,8},{24,16},{9,1},{17,9},{25,17},{10,2},{18,10},{26,18},{... | collective-permute-start | bytes 1253384 | tf_op jit(solution)/shard_map/ppermute | solution.py:19
  186.3 7.9 %collective-permute-start.6 = (f32[17,16,3,128]{3,1,2,0:T(8,128)S(1)}, f32[17,16,3,128]{3,1,2,0:T(8,128)S(1)}, u32[]{:S(2)}, u32[]{:S(2)}) collective-permute-start(f32[17,16,3,128]{3,1,2,0:T(8,128)S(1)} %get-tuple-element.45), channel_id=1, source_target_pairs={{0,8},{8,16},{16,24},{1,9},{9,17},{17,25},{2,10},{10,18},{18,26},{... | collective-permute-start | bytes 1253384 | tf_op jit(solution)/shard_map/ppermute | solution.py:16
  188.8 9.9 %collective-permute-start.7 = (f32[17,16,3,128]{3,1,2,0:T(8,128)S(1)}, f32[17,16,3,128]{3,1,2,0:T(8,128)S(1)}, u32[]{:S(2)}, u32[]{:S(2)}) collective-permute-start(f32[17,16,3,128]{3,1,2,0:T(8,128)S(1)} %get-tuple-element.46), channel_id=1, source_target_pairs={{8,0},{16,8},{24,16},{9,1},{17,9},{25,17},{10,2},{18,10},{26,18},{... | collective-permute-start | bytes 1253384 | tf_op jit(solution)/shard_map/ppermute | solution.py:19
  199.5 0.8 copy-start.16
  199.5 3.5 %copy-start.1 = (bf16[256,256]{1,0:T(8,128)(2,1)S(1)}, bf16[256,256]{1,0:T(8,128)(2,1)}, u32[]{:S(2)}) copy-start(bf16[256,256]{1,0:T(8,128)(2,1)} %param.19) | copy-start | bytes 393220
where the time goes:
time: 205 us; the launch traced here: 203 us
  local copies, waits for them, and re-layouts  112 us (55%)
  waiting for transfers between devices  30.6 us (15%)
  other arithmetic  30.1 us (15%)
  starting transfers between devices  27.4 us (13%)
    scatter x1, local copies, waits for them, and re-layouts, on_device(): places = jnp.zeros((device_count, capacity), jnp.float32).at[owner_tile,...  66.6 us
    scatter x2, local copies, waits for them, and re-layouts, on_device(): outgoing = jnp.zeros((device_count, capacity, tracer_count), jnp.float32)...  24.4 us
    ppermute x4, waiting for transfers between devices, with_halo(): lax.ppermute(lax.slice_in_dim(block, block.shape[dim] - width, None, axis...  14.9 us
    ppermute x4, starting transfers between devices, with_halo(): lax.ppermute(lax.slice_in_dim(block, 0, width, axis=dim), axis, backward)  8.6 us
    ppermute x4, waiting for transfers between devices, with_halo(): lax.ppermute(lax.slice_in_dim(block, 0, width, axis=dim), axis, backward)  8.45 us
    all_to_all x1, starting transfers between devices, on_device(): lax.all_to_all(places, ('lat', 'lon'), split_axis=0, concat_axis=0, tiled...  7.86 us
    all_to_all x1, waiting for transfers between devices, on_device(): lax.all_to_all(outgoing, ('lat', 'lon'), split_axis=0, concat_axis=0, til...  7.26 us
    scatter-add x1, other arithmetic, on_device(): emitted = jnp.zeros((tile_rows * tile_cols, tracer_count), jnp.float32).a...  6.67 us
  transfers between devices with their start and end apart: 10, of which 7 were waited for; matrix products, arithmetic and copies ran while one was open for 17% of the time, Pallas kernels for 0%

commit v1 on v0

v1 whole, which is shorter than its diff:
```python
import functools

import jax
import jax.numpy as jnp
from jax import lax
from jax.experimental import pallas as pl
from jax.experimental.pallas import tpu as pltpu
from jax.sharding import PartitionSpec as P

MESH = pl.DeviceIdType.MESH
LANES = 128
WIDE = 6


def silu(v):
    return v / (1.0 + jnp.exp(-v))


def face_weights(c):
    p = jnp.maximum(c, 0.0)
    w = jnp.maximum(-c, 0.0)
    alpha = 0.5 * p * p
    beta = 1.0 - 2.0 / 3.0 * p
    gamma = 0.5 * w * w
    delta = 1.0 - 2.0 / 3.0 * w
    x = alpha * (1.0 - 3.0 * beta)
    y = c - alpha * (1.0 + 3.0 * beta) + gamma * (1.0 + 3.0 * delta)
    z = -gamma * (1.0 - 3.0 * delta)
    u = 6.0 * alpha * beta
    v = -6.0 * gamma * delta
    a, b = 7.0 / 12.0, 1.0 / 12.0
    return [
        -b * x,
        a * x - b * y,
        a * (x + y) - b * z + u,
        a * (y + z) - b * x + v,
        a * z - b * y,
        -b * z,
    ]


def cell_weights(c, before):
    f, g = face_weights(c), face_weights(before)
    out = [g[0]]
    for m in range(5):
        out.append(g[m + 1] - f[m])
    out.append(-f[5])
    out[3] = out[3] + 1.0
    return out


def kernel(
    n_lat,
    n_lon,
    cap,
    feat_ref,
    tile_ref,
    spot_ref,
    w_in_ref,
    b_in_ref,
    w_mid_ref,
    b_mid_ref,
    w_out_ref,
    x_ref,
    zon_ref,
    mer_ref,
    mix_ref,
    out_ref,
    lon_out,
    lon_in,
    lon0_out,
    lon0_in,
    mer_in,
    route_out,
    route_in,
    gz,
    gze,
    gm,
    st,
    fin,
    lon_sem,
    lon0_sem,
    mer_sem,
    route_send,
    route_recv,
    lat_send,
    lat_recv,
):
    lev, rows, _ = zon_ref.shape
    cells = feat_ref.shape[0]
    tr = st.shape[2]
    per = lev * rows
    count = n_lat * n_lon
    groups = LANES // cap
    blocks = count // groups
    lat, lon = lax.axis_index("lat"), lax.axis_index("lon")
    me = lat * n_lon + lon
    west, east = lax.rem(lon + n_lon - 1, n_lon), lax.rem(lon + 1, n_lon)
    has_south, has_north = lat > 0, lat < n_lat - 1

    def place(d):
        return lax.rem(d, groups) * blocks + d // groups

    barrier = pltpu.get_barrier_semaphore()

    @pl.loop(1, count)
    def _(o):
        d = lax.rem(me + o, count)
        pl.semaphore_signal(
            barrier, inc=1, device_id=(d // n_lon, lax.rem(d, n_lon)), device_id_type=MESH
        )

    lane = lax.broadcasted_iota(jnp.int32, (tr, LANES), 1)
    lane8 = lax.broadcasted_iota(jnp.int32, (rows, LANES), 1)

    def column(k, a):
        return x_ref[pl.ds(k * rows + a, tr, stride=per), :]

    @pl.loop(0, lev // 2)
    def _(kp):
        left = jnp.zeros((tr, LANES), jnp.float32)
        right = left
        for p in range(2 * rows):
            q = column(2 * kp + p // rows, p % rows)
            mine = lane // 8 == p
            left = jnp.where(mine, pltpu.roll(q, 8 * p, 1), left)
            right = jnp.where(mine, pltpu.roll(q, (8 * p + 8) % LANES, 1), right)
        lon_out[0, pl.ds(2 * kp, 2)] = left.reshape(2, 8, LANES)
        lon_out[1, pl.ds(2 * kp, 2)] = right.reshape(2, 8, LANES)

    left = jnp.zeros((rows, LANES), jnp.float32)
    right = left
    for k in range(lev):
        c = zon_ref[k]
        mine = lane8 // 8 == k
        left = jnp.where(mine, pltpu.roll(c, (8 * k) % LANES, 1), left)
        right = jnp.where(mine, pltpu.roll(c, (8 * k + 8) % LANES, 1), right)
    lon_out[0, lev] = left
    lon_out[1, lev] = right

    pl.semaphore_wait(barrier, count - 1)

    def lon_copy(side):
        return pltpu.make_async_remote_copy(
            src_ref=lon_out.at[side],
            dst_ref=lon_in.at[side],
            send_sem=lon_sem.at[0, side],
            recv_sem=lon_sem.at[1, side],
            device_id=(lat, (west, east)[side]),
            device_id_type=MESH,
        )

    def lon0_copy(side):
        return pltpu.make_async_remote_copy(
            src_ref=lon0_out.at[side],
            dst_ref=lon0_in.at[side],
            send_sem=lon0_sem.at[0, side],
            recv_sem=lon0_sem.at[1, side],
            device_id=(lat, (west, east)[side]),
            device_id_type=MESH,
        )

    def mer_copy(side):
        return pltpu.make_async_remote_copy(
            src_ref=mer_ref,
            dst_ref=mer_in.at[side],
            send_sem=mer_sem.at[0, side],
            recv_sem=mer_sem.at[1, side],
            device_id=(lat + (-1, 1)[side], lon),
            device_id_type=MESH,
        )

    def lat_copy(k, side):
        return pltpu.make_async_remote_copy(
            src_ref=st.at[k, pl.ds((WIDE, rows)[side], WIDE)],
            dst_ref=st.at[k, pl.ds((WIDE + rows, 0)[side], WIDE)],
            send_sem=lat_send.at[side, k],
            recv_sem=lat_recv.at[side, k],
            device_id=(lat + (-1, 1)[side], lon),
            device_id_type=MESH,
        )

    def route_copy(d, origin):
        return pltpu.make_async_remote_copy(
            src_ref=route_out.at[place(d)],
            dst_ref=route_in.at[place(origin)],
            send_sem=route_send.at[d],
            recv_sem=route_recv.at[origin],
            device_id=(d // n_lon, lax.rem(d, n_lon)),
            device_id_type=MESH,
        )

    lon_copy(0).start()
    lon_copy(1).start()

    @pl.when(has_south)
    def _():
        mer_copy(0).start()

    @pl.when(has_north)
    def _():
        mer_copy(1).start()

    @pl.when(jnp.logical_not(has_south))
    def _():
        mer_in[1] = jnp.zeros((lev, rows, LANES), jnp.float32)

        @pl.loop(0, lev)
        def _(k):
            st[k, 0:WIDE] = jnp.zeros((WIDE, tr, LANES), jnp.float32)

    @pl.when(jnp.logical_not(has_north))
    def _():
        mer_in[0] = jnp.zeros((lev, rows, LANES), jnp.float32)

        @pl.loop(0, lev)
        def _(k):
            st[k, WIDE + rows :] = jnp.zeros((WIDE, tr, LANES), jnp.float32)

    first = silu(
        jnp.dot(feat_ref[...], w_in_ref[...], preferred_element_type=jnp.float32) + b_in_ref[...]
    ).astype(jnp.bfloat16)
    second = silu(
        jnp.dot(first, w_mid_ref[...], preferred_element_type=jnp.float32) + b_mid_ref[...]
    ).astype(jnp.bfloat16)
    flux = lax.dot_general(
        w_out_ref[...], second, (((0,), (1,)), ((), ())), preferred_element_type=jnp.float32
    )

    tile = tile_ref[...]
    named = (tile == lax.broadcasted_iota(jnp.int32, (cells, LANES), 1)).astype(jnp.float32)
    ahead = (
        lax.broadcasted_iota(jnp.int32, (cells, cells), 0)
        > lax.broadcasted_iota(jnp.int32, (cells, cells), 1)
    ).astype(jnp.float32)
    rank = jnp.dot(
        ahead.astype(jnp.bfloat16), named.astype(jnp.bfloat16), preferred_element_type=jnp.float32
    )
    slot = jnp.sum(rank * named, axis=1, keepdims=True).astype(jnp.int32)
    key = tile * cap + slot
    taken = (key == lax.broadcasted_iota(jnp.int32, (cells, count * cap), 1)).astype(jnp.float32)
    spot = spot_ref[...]
    spots = jnp.where(
        lax.broadcasted_iota(jnp.int32, (16, cells), 0) == 0, spot // LANES, spot % LANES
    ).astype(jnp.float32)
    high = flux.astype(jnp.bfloat16)
    low = (flux - high.astype(jnp.float32)).astype(jnp.bfloat16)
    parts = jnp.concatenate([high, low, spots.astype(jnp.bfloat16)], axis=0)
    placed = jnp.dot(parts, taken.astype(jnp.bfloat16), preferred_element_type=jnp.float32)
    summed = placed[0:tr] + placed[tr : 2 * tr]
    pieces = [summed[0:8], summed[8:16], placed[2 * tr : 2 * tr + 8]]
    stacked = [
        jnp.concatenate([piece[:, LANES * j : LANES * (j + 1)] for j in range(blocks)], axis=0)
        for piece in pieces
    ]
    laneb = lax.broadcasted_iota(jnp.int32, (8 * blocks, LANES), 1)
    for g in range(groups):
        turned = [
            pltpu.roll(s, (cap * (h - g)) % LANES, 1) if h != g else s
            for h, s in enumerate(stacked)
        ]
        packed = jnp.where(laneb < cap, turned[0], jnp.where(laneb < 2 * cap, turned[1], turned[2]))
        route_out[blocks * g : blocks * (g + 1)] = packed.reshape(blocks, 8, LANES)

    @pl.loop(1, count)
    def _(o):
        route_copy(lax.rem(me + o, count), me).start()

    route_in[place(me)] = route_out[place(me)]

    lon_copy(0).wait_recv()
    lon_copy(1).wait_recv()

    def ring(main, ext, m, where):
        if m == 0:
            return main, ext
        if m > 0:
            mask, turn = where < m, LANES - m
        else:
            mask, turn = where >= LANES + m, -m
        return (
            pltpu.roll(jnp.where(mask, ext, main), turn, 1),
            pltpu.roll(jnp.where(mask, main, ext), turn, 1),
        )

    def unpack(from_west, from_east, p, where):
        return jnp.where(
            where < 8,
            pltpu.roll(from_east, (LANES - 8 * p) % LANES, 1),
            pltpu.roll(from_west, (LANES - 8 - 8 * p) % LANES, 1),
        )

    for k in range(lev):
        c = zon_ref[k]
        ce = unpack(lon_in[1, lev], lon_in[0, lev], k, lane8)
        before, before_e = ring(c, ce, -1, lane8)
        for m, weight in enumerate(cell_weights(c, before)):
            gz[k, m] = weight
        for m, weight in enumerate(cell_weights(ce, before_e)):
            gze[k, m] = weight

    def zonal(k, a, main, ext):
        new, new_e = 0.0, 0.0
        for m in range(-3, 4):
            near, near_e = ring(main, ext, m, lane)
            new = new + near * gz[k, m + 3, a : a + 1, :]
            new_e = new_e + near_e * gze[k, m + 3, a : a + 1, :]
        main, ext = new, new_e
        new = 0.0
        for m in range(-3, 4):
            if m == 0:
                near = main
            elif m > 0:
                near = pltpu.roll(jnp.where(lane < m, ext, main), LANES - m, 1)
            else:
                near = pltpu.roll(jnp.where(lane >= LANES + m, ext, main), -m, 1)
            new = new + near * gz[k, m + 3, a : a + 1, :]
        st[k, WIDE + a] = new

    def send_rows(k):
        @pl.when(has_south)
        def _():
            lat_copy(k, 0).start()

        @pl.when(has_north)
        def _():
            lat_copy(k, 1).start()

    def pair(kp, parities):
        from_west = lon_in[1, pl.ds(2 * kp, 2)].reshape(tr, LANES)
        from_east = lon_in[0, pl.ds(2 * kp, 2)].reshape(tr, LANES)
        for parity in parities:
            k = 2 * kp + parity
            for a in range(rows):
                ext = unpack(from_west, from_east, parity * rows + a, lane)
                zonal(k, a, column(k, a), ext)
            send_rows(k)

    pair(0, (1,))

    @pl.loop(1, lev // 2)
    def _(kp):
        pair(kp, (0, 1))

    @pl.loop(1, count)
    def _(o):
        route_copy(me, lax.rem(me + o, count)).wait_recv()

    lists = [jnp.zeros((8 * blocks, LANES), jnp.float32)] * 3
    for g in range(groups):
        got = route_in[blocks * g : blocks * (g + 1)].reshape(8 * blocks, LANES)
        for h in range(3):
            turned = pltpu.roll(got, (cap * (g - h)) % LANES, 1) if g != h else got
            lists[h] = jnp.where(laneb // cap == g, turned, lists[h])
    entries = [
        jnp.concatenate([part[8 * j : 8 * (j + 1)] for j in range(blocks)], axis=1)
        for part in lists
    ]
    values = jnp.concatenate(entries[:2], axis=0)
    at_row, at_lane = entries[2][0:1], entries[2][1:2]
    wide = blocks * LANES
    onto = (
        lax.broadcasted_iota(jnp.int32, (LANES, wide), 0).astype(jnp.float32) == at_lane
    ).astype(jnp.float32)
    spread = jnp.concatenate(
        [jnp.where(at_row == float(a), values, 0.0) for a in range(rows)], axis=0
    )
    high = spread.astype(jnp.bfloat16)
    low = (spread - high.astype(jnp.float32)).astype(jnp.bfloat16)
    emitted = lax.dot_general(
        jnp.concatenate([high, low], axis=0),
        onto.astype(jnp.bfloat16),
        (((1,), (1,)), ((), ())),
        preferred_element_type=jnp.float32,
    )
    emitted = emitted[: rows * tr] + emitted[rows * tr :]

    surface = [column(0, a) + emitted[a * tr : (a + 1) * tr] for a in range(rows)]
    left = jnp.zeros((tr, LANES), jnp.float32)
    right = left
    for a in range(rows):
        mine = lane // 8 == a
        left = jnp.where(mine, pltpu.roll(surface[a], 8 * a, 1), left)
        right = jnp.where(mine, pltpu.roll(surface[a], 8 * a + 8, 1), right)
        fin[0, a] = surface[a]
    lon0_out[0] = left
    lon0_out[1] = right
    lon0_copy(0).start()
    lon0_copy(1).start()

    @pl.when(has_south)
    def _():
        mer_copy(1).wait_recv()

    @pl.when(has_north)
    def _():
        mer_copy(0).wait_recv()

    grid_row = lax.broadcasted_iota(jnp.int32, (3 * rows, LANES), 0) + (lat - 1) * rows
    northern = (grid_row < n_lat * rows - 1).astype(jnp.float32)

    @pl.loop(0, lev)
    def _(k):
        c = jnp.concatenate([mer_in[1, k], mer_ref[k], mer_in[0, k]], axis=0) * northern
        for m, weight in enumerate(cell_weights(c, pltpu.roll(c, 1, 0))):
            gm[k, m] = weight

    lon0_copy(0).wait_recv()
    lon0_copy(1).wait_recv()
    for a in range(rows):
        zonal(0, a, fin[0, a], unpack(lon0_in[1], lon0_in[0], a, lane))
    send_rows(0)

    def meridional(k):
        @pl.when(has_south)
        def _():
            lat_copy(k, 1).wait_recv()

        @pl.when(has_north)
        def _():
            lat_copy(k, 0).wait_recv()

        for h in range(0, tr, 8):
            once = []
            for a in range(-3, rows + 3):
                new = 0.0
                for m in range(7):
                    new = new + st[k, a + 3 + m, h : h + 8] * gm[k, m, a + rows : a + rows + 1]
                once.append(new)
            for a in range(rows):
                new = 0.0
                for m in range(7):
                    new = new + once[a + m] * gm[k, m, a + rows : a + rows + 1]
                fin[k, a, h : h + 8] = new

    @pl.loop(1, lev)
    def _(k):
        meridional(k)

    meridional(0)

    @pl.loop(0, rows)
    def _(a):
        for h in range(0, tr, 8):
            held = [fin[j, a, h : h + 8] for j in range(lev)]
            for k in range(lev):
                total = held[0] * mix_ref[a, k, 0]
                for j in range(1, lev):
                    total = total + held[j] * mix_ref[a, k, j]
                out_ref[pl.ds(h * per + k * rows + a, 8, stride=per), :] = total

    for side in range(2):
        lon_copy(side).wait_send()
        lon0_copy(side).wait_send()

    @pl.loop(1, count)
    def _(o):
        route_copy(lax.rem(me + o, count), me).wait_send()

    @pl.when(has_south)
    def _():
        mer_copy(0).wait_send()

        @pl.loop(0, lev)
        def _(k):
            lat_copy(k, 0).wait_send()

    @pl.when(has_north)
    def _():
        mer_copy(1).wait_send()

        @pl.loop(0, lev)
        def _(k):
            lat_copy(k, 1).wait_send()


def on_device(
    n_lat,
    n_lon,
    features,
    land_tile,
    land_spot,
    w_in,
    b_in,
    w_mid,
    b_mid,
    w_out,
    tracers,
    zonal_wind,
    meridional_wind,
    mixing,
):
    tr, lev, rows, cols = tracers.shape
    cells = features.shape[0]
    count = n_lat * n_lon
    cap = 2 * cells // count
    f32 = jnp.float32
    vmem = pl.BlockSpec(memory_space=pltpu.VMEM)
    smem = pl.BlockSpec(memory_space=pltpu.SMEM)
    out = pl.pallas_call(
        functools.partial(kernel, n_lat, n_lon, cap),
        out_shape=jax.ShapeDtypeStruct((tr * lev * rows, cols), f32),
        in_specs=[vmem] * 11 + [smem],
        out_specs=vmem,
        scratch_shapes=[
            pltpu.VMEM((2, lev + 1, 8, cols), f32),
            pltpu.VMEM((2, lev + 1, 8, cols), f32),
            pltpu.VMEM((2, tr, cols), f32),
            pltpu.VMEM((2, tr, cols), f32),
            pltpu.VMEM((2, lev, rows, cols), f32),
            pltpu.VMEM((count, 8, cols), f32),
            pltpu.VMEM((count, 8, cols), f32),
            pltpu.VMEM((lev, 7, rows, cols), f32),
            pltpu.VMEM((lev, 7, rows, cols), f32),
            pltpu.VMEM((lev, 7, 3 * rows, cols), f32),
            pltpu.VMEM((lev, rows + 2 * WIDE, tr, cols), f32),
            pltpu.VMEM((lev, rows, tr, cols), f32),
            pltpu.SemaphoreType.DMA((2, 2)),
            pltpu.SemaphoreType.DMA((2, 2)),
            pltpu.SemaphoreType.DMA((2, 2)),
            pltpu.SemaphoreType.DMA((count,)),
            pltpu.SemaphoreType.DMA((count,)),
            pltpu.SemaphoreType.DMA((2, lev)),
            pltpu.SemaphoreType.DMA((2, lev)),
        ],
        compiler_params=pltpu.CompilerParams(
            collective_id=0, has_side_effects=True, vmem_limit_bytes=40 * 1024 * 1024
        ),
    )(
        features,
        land_tile,
        land_spot.reshape(1, -1),
        w_in,
        b_in.reshape(1, -1),
        w_mid,
        b_mid.reshape(1, -1),
        w_out,
        tracers.reshape(tr * lev * rows, cols),
        zonal_wind,
        meridional_wind,
        mixing,
    )
    return out.reshape(tr, lev, rows, cols)


def solution(mesh):
    placed = (
        P(("lat", "lon"), None),
        P(("lat", "lon"), None),
        P(("lat", "lon")),
        P(),
        P(),
        P(),
        P(),
        P(),
        P(None, None, "lat", "lon"),
        P(None, "lat", "lon"),
        P(None, "lat", "lon"),
        P("lat", None, None),
    )
    return jax.shard_map(
        functools.partial(on_device, mesh.shape["lat"], mesh.shape["lon"]),
        mesh=mesh,
        in_specs=placed,
        out_specs=P(None, None, "lat", "lon"),
        check_vma=False,
    )
```

time: 205 us -> 46.7 us (0.23)
  local copies, waits for them, and re-layouts: 112 us -> 4.6 us
  Pallas kernels: 0 us -> 41.8 us
  waiting for transfers between devices: 30.6 us -> 0 us
  other arithmetic: 30.1 us -> 0 us
  starting transfers between devices: 27.4 us -> 0 us
    scatter x3 -> x0, local copies, waits for them, and re-layouts: 91 us -> none  [the longest x1 66.6 us: on_device(): places = jnp.zeros((device_count, capacity), jnp.float32).at[owner_tile,...]
    pallas_call x0 -> x1, Pallas kernels: none -> 41.8 us  [on_device(): pl.pallas_call(functools.partial(kernel, n_lat, n_lon, cap), out_shape=ja...]
    ppermute x8 -> x0, waiting for transfers between devices: 23.3 us -> none  [the longest x4 14.9 us: with_halo(): lax.ppermute(lax.slice_in_dim(block, block.shape[dim] - width, None, axis...]
    all_to_all x2 -> x0, starting transfers between devices: 13.7 us -> none  [the longest x1 7.86 us: on_device(): lax.all_to_all(places, ('lat', 'lon'), split_axis=0, concat_axis=0, tiled...]
    ppermute x8 -> x0, starting transfers between devices: 13.7 us -> none  [the longest x4 8.6 us: with_halo(): lax.ppermute(lax.slice_in_dim(block, 0, width, axis=dim), axis, backward)]
    all_to_all x2 -> x0, waiting for transfers between devices: 7.26 us -> none  [the longest x1 7.26 us: on_device(): lax.all_to_all(outgoing, ('lat', 'lon'), split_axis=0, concat_axis=0, til...]
    ppermute x4 -> x0, local copies, waits for them, and re-layouts: 6.94 us -> none  [the longest x2 4.41 us: with_halo(): lax.ppermute(lax.slice_in_dim(block, 0, width, axis=dim), axis, backward)]
    sub x11 -> x0, other arithmetic: 6.79 us -> none  [the longest x4 3.06 us: transport(): 7.0 / 12.0 * (section(values, 1, -2, axis) + section(values, 2, -1, axis))]
  transfers between devices with their start and end apart: 10 -> 0, of which waited for: 7 -> 0; matrix products, arithmetic and copies ran while one was open for 17% -> 0% of each run, Pallas kernels for 0% -> 0%
where the time goes in v1:
time: 46.7 us; the launch traced here: 46.4 us
  Pallas kernels  41.8 us (90%)
  local copies, waits for them, and re-layouts  4.6 us (10%)
    pallas_call x1, Pallas kernels, on_device(): pl.pallas_call(functools.partial(kernel, n_lat, n_lon, cap), out_shape=ja...  41.8 us
    unnamed x26, local copies, waits for them, and re-layouts  4.6 us

profile of v1, /device:TPU:0, one launch (start us, length us, event | category | flops | bytes accessed | tf_op | source)
XLA Modules:
  0.0 46.4 jit_solution(17232692485483099909)
XLA Ops:
  0.0 0.0 copy-start.9
  0.0 0.8 %copy.15.w_out_ref = bf16[256,16]{1,0:T(8,128)(2,1)S(1)} copy(bf16[256,16]{0,1:T(8,128)(2,1)} %param.19) | data formatting | bytes 16384 | tf_op args[7]
  0.9 0.0 copy-done.9
  0.9 0.0 copy-start.10
  0.9 0.0 copy-start.4
  0.9 0.0 copy-start.5
  0.9 0.0 copy-start.7
  0.9 0.0 copy-start.8
  0.9 0.1 copy.13.feat_ref
  1.0 0.5 %copy-done.10 = s32[512,1]{0,1:T(1,128)S(1)} copy-done((s32[512,1]{0,1:T(1,128)S(1)}, s32[512,1]{0,1:T(1,128)}, u32[]{:S(2)}) %copy-start.10) | copy-done | bytes 2072
  1.5 0.0 copy-start.1
  1.5 0.0 copy-start.2
  1.5 0.0 copy-start.3
  1.5 0.0 copy-start.6
  1.6 0.1 copy.14.tile_ref
  1.7 0.0 copy-done.4
  1.7 0.0 copy-done.5
  1.7 0.0 copy-done.7
  1.7 0.0 copy-done.8
  1.7 0.7 %copy-done.1 = bf16[256,256]{1,0:T(8,128)(2,1)S(1)} copy-done((bf16[256,256]{1,0:T(8,128)(2,1)S(1)}, bf16[256,256]{1,0:T(8,128)(2,1)}, u32[]{:S(2)}) %copy-start.1) | copy-done | bytes 131096
  2.5 0.0 copy-done.2
  2.5 0.0 copy-done.3
  2.5 0.0 copy-done.6
  2.5 0.0 copy-start
  2.5 1.2 %copy-done = f32[16,16,8,128]{3,2,1,0:T(8,128)S(1)} copy-done((f32[16,16,8,128]{3,2,1,0:T(8,128)S(1)}, f32[16,16,8,128]{3,2,1,0:T(8,128)}, u32[]{:S(2)}) %copy-start) | copy-done | bytes 1048600
  3.7 41.8 %shard_map.118 = f32[2048,128]{1,0:T(8,128)S(1)} custom-call(bf16[512,64]{1,0:T(8,128)(2,1)S(1)} %copy.13.feat_ref, s32[512,1]{1,0:T(8,128)S(1)} %copy.14.tile_ref, s32[1,512]{1,0:T(1,128)S(1)} %bitcast.7, bf16[64,256]{1,0:T(8,128)(2,1)S(1)} %copy-done.5, f32[1,256]{1,0:T(1,128)S(1)} %bitcast.8, bf16[256,256]{1,0:T(8,128)(2,1)S(1)} %copy-done.1, ...), custom_call_target="tpu_custom_call" | custom-call | tf_op jit(solution)/shard_map/pallas_call | solution.py:500
  45.5 1.0 %copy.17 = f32[16,16,8,128]{3,2,1,0:T(8,128)} copy(f32[16,16,8,128]{3,2,1,0:T(8,128)S(1)} %bitcast.5) | data formatting | bytes 2097152
Async XLA Ops:
  0.0 0.9 %copy-start.9 = (bf16[512,64]{0,1:T(8,128)(2,1)S(1)}, bf16[512,64]{0,1:T(8,128)(2,1)}, u32[]{:S(2)}) copy-start(bf16[512,64]{0,1:T(8,128)(2,1)} %param.12) | copy-start | bytes 196612
  0.9 0.7 %copy-start.10 = (s32[512,1]{0,1:T(1,128)S(1)}, s32[512,1]{0,1:T(1,128)}, u32[]{:S(2)}) copy-start(s32[512,1]{0,1:T(1,128)} %param.13) | copy-start | bytes 6148
  0.9 0.8 %copy-start.4 = (f32[8,16,16]{2,1,0:T(8,128)S(1)}, f32[8,16,16]{2,1,0:T(8,128)}, u32[]{:S(2)}) copy-start(f32[8,16,16]{2,1,0:T(8,128)} %mix_ref.1) | copy-start | bytes 24580
  0.9 0.8 %copy-start.5 = (bf16[64,256]{1,0:T(8,128)(2,1)S(1)}, bf16[64,256]{1,0:T(8,128)(2,1)}, u32[]{:S(2)}) copy-start(bf16[64,256]{1,0:T(8,128)(2,1)} %w_in_ref.1) | copy-start | bytes 98308
  0.9 0.8 %copy-start.7 = (f32[256]{0:T(256)S(1)}, f32[256]{0:T(256)}, u32[]{:S(2)}) copy-start(f32[256]{0:T(256)} %param.16) | copy-start | bytes 3076
  0.9 0.8 %copy-start.8 = (f32[256]{0:T(256)S(1)}, f32[256]{0:T(256)}, u32[]{:S(2)}) copy-start(f32[256]{0:T(256)} %param.18) | copy-start | bytes 3076
  1.5 0.9 %copy-start.1 = (bf16[256,256]{1,0:T(8,128)(2,1)S(1)}, bf16[256,256]{1,0:T(8,128)(2,1)}, u32[]{:S(2)}) copy-start(bf16[256,256]{1,0:T(8,128)(2,1)} %w_mid_ref.1) | copy-start | bytes 393220
  1.5 0.9 %copy-start.2 = (f32[16,8,128]{2,1,0:T(8,128)S(1)}, f32[16,8,128]{2,1,0:T(8,128)}, u32[]{:S(2)}) copy-start(f32[16,8,128]{2,1,0:T(8,128)} %zon_ref.1) | copy-start | bytes 196612
  1.5 0.9 %copy-start.3 = (f32[16,8,128]{2,1,0:T(8,128)S(1)}, f32[16,8,128]{2,1,0:T(8,128)}, u32[]{:S(2)}) copy-start(f32[16,8,128]{2,1,0:T(8,128)} %mer_ref.1) | copy-start | bytes 196612
  1.5 0.9 %copy-start.6 = (s32[512]{0:T(512)S(1)}, s32[512]{0:T(512)}, u32[]{:S(2)}) copy-start(s32[512]{0:T(512)} %param.14) | copy-start | bytes 6148
  2.5 1.2 %copy-start = (f32[16,16,8,128]{3,2,1,0:T(8,128)S(1)}, f32[16,16,8,128]{3,2,1,0:T(8,128)}, u32[]{:S(2)}) copy-start(f32[16,16,8,128]{3,2,1,0:T(8,128)} %param.20) | copy-start | bytes 3145732

commit v2 on v1

--- a/solution.py
+++ b/solution.py
@@ -53,19 +53,21 @@
     n_lat,
     n_lon,
     cap,
-    feat_ref,
-    tile_ref,
-    spot_ref,
-    w_in_ref,
-    b_in_ref,
-    w_mid_ref,
-    b_mid_ref,
-    w_out_ref,
-    x_ref,
-    zon_ref,
-    mer_ref,
-    mix_ref,
+    *refs,
+):
+    given, refs = refs[:12], refs[12:]
+    out_ref, held, refs = refs[0], refs[1:13], refs[13:]
+    transport_step(n_lat, n_lon, cap, given, held, out_ref, *refs)
+
+
+def transport_step(
+    n_lat,
+    n_lon,
+    cap,
+    given,
+    held,
     out_ref,
+    given_sem,
     lon_out,
     lon_in,
     lon0_out,
@@ -78,6 +80,8 @@
     gm,
     st,
     fin,
+    acc,
+    slots,
     lon_sem,
     lon0_sem,
     mer_sem,
@@ -86,8 +90,22 @@
     lat_send,
     lat_recv,
 ):
+    (
+        feat_ref,
+        tile_ref,
+        spot_ref,
+        w_in_ref,
+        b_in_ref,
+        w_mid_ref,
+        b_mid_ref,
+        w_out_ref,
+        x_ref,
+        zon_ref,
+        mer_ref,
+        mix_ref,
+    ) = held
     lev, rows, _ = zon_ref.shape
-    cells = feat_ref.shape[0]
+    cells = feat_ref.shape[1]
     tr = st.shape[2]
     per = lev * rows
     count = n_lat * n_lon
@@ -101,6 +119,12 @@
     def place(d):
         return lax.rem(d, groups) * blocks + d // groups
 
+    def load(i):
+        return pltpu.make_async_copy(given[i], held[i], given_sem.at[i])
+
+    for i in (8, 9, 10, 0, 3, 5, 4, 6, 7, 1, 2, 11):
+        load(i).start()
+
     barrier = pltpu.get_barrier_semaphore()
 
     @pl.loop(1, count)
@@ -115,6 +139,24 @@
 
     def column(k, a):
         return x_ref[pl.ds(k * rows + a, tr, stride=per), :]
+
+    @pl.when(jnp.logical_not(has_south))
+    def _():
+        mer_in[1] = jnp.zeros((lev, rows, LANES), jnp.float32)
+
+        @pl.loop(0, lev)
+        def _(k):
+            st[k, 0:WIDE] = jnp.zeros((WIDE, tr, LANES), jnp.float32)
+
+    @pl.when(jnp.logical_not(has_north))
+    def _():
+        mer_in[0] = jnp.zeros((lev, rows, LANES), jnp.float32)
+
+        @pl.loop(0, lev)
+        def _(k):
+            st[k, WIDE + rows :] = jnp.zeros((WIDE, tr, LANES), jnp.float32)
+
+    load(8).wait()
 
     @pl.loop(0, lev // 2)
     def _(kp):
@@ -122,12 +164,14 @@
         right = left
         for p in range(2 * rows):
             q = column(2 * kp + p // rows, p % rows)
+            st[2 * kp + p // rows, WIDE + p % rows] = q
             mine = lane // 8 == p
             left = jnp.where(mine, pltpu.roll(q, 8 * p, 1), left)
             right = jnp.where(mine, pltpu.roll(q, (8 * p + 8) % LANES, 1), right)
         lon_out[0, pl.ds(2 * kp, 2)] = left.reshape(2, 8, LANES)
         lon_out[1, pl.ds(2 * kp, 2)] = right.reshape(2, 8, LANES)
 
+    load(9).wait()
     left = jnp.zeros((rows, LANES), jnp.float32)
     right = left
     for k in range(lev):
@@ -192,6 +236,7 @@
 
     lon_copy(0).start()
     lon_copy(1).start()
+    load(10).wait()
 
     @pl.when(has_south)
     def _():
@@ -201,72 +246,20 @@
     def _():
         mer_copy(1).start()
 
-    @pl.when(jnp.logical_not(has_south))
-    def _():
-        mer_in[1] = jnp.zeros((lev, rows, LANES), jnp.float32)
-
-        @pl.loop(0, lev)
-        def _(k):
-            st[k, 0:WIDE] = jnp.zeros((WIDE, tr, LANES), jnp.float32)
-
-    @pl.when(jnp.logical_not(has_north))
-    def _():
-        mer_in[0] = jnp.zeros((lev, rows, LANES), jnp.float32)
-
-        @pl.loop(0, lev)
-        def _(k):
-            st[k, WIDE + rows :] = jnp.zeros((WIDE, tr, LANES), jnp.float32)
-
+    for i in (0, 3, 5, 4, 6, 7, 1, 2):
+        load(i).wait()
     first = silu(
-        jnp.dot(feat_ref[...], w_in_ref[...], preferred_element_type=jnp.float32) + b_in_ref[...]
+        lax.dot_general(
+            feat_ref[...], w_in_ref[...], (((0,), (0,)), ((), ())), preferred_element_type=jnp.float32
+        )
+        + b_in_ref[...]
     ).astype(jnp.bfloat16)
     second = silu(
         jnp.dot(first, w_mid_ref[...], preferred_element_type=jnp.float32) + b_mid_ref[...]
     ).astype(jnp.bfloat16)
     flux = lax.dot_general(
-        w_out_ref[...], second, (((0,), (1,)), ((), ())), preferred_element_type=jnp.float32
+        w_out_ref[...], second, (((1,), (1,)), ((), ())), preferred_element_type=jnp.float32
     )
-
-    tile = tile_ref[...]
-    named = (tile == lax.broadcasted_iota(jnp.int32, (cells, LANES), 1)).astype(jnp.float32)
-    ahead = (
-        lax.broadcasted_iota(jnp.int32, (cells, cells), 0)
-        > lax.broadcasted_iota(jnp.int32, (cells, cells), 1)
-    ).astype(jnp.float32)
-    rank = jnp.dot(
-        ahead.astype(jnp.bfloat16), named.astype(jnp.bfloat16), preferred_element_type=jnp.float32
-    )
-    slot = jnp.sum(rank * named, axis=1, keepdims=True).astype(jnp.int32)
-    key = tile * cap + slot
-    taken = (key == lax.broadcasted_iota(jnp.int32, (cells, count * cap), 1)).astype(jnp.float32)
-    spot = spot_ref[...]
-    spots = jnp.where(
-        lax.broadcasted_iota(jnp.int32, (16, cells), 0) == 0, spot // LANES, spot % LANES
-    ).astype(jnp.float32)
-    high = flux.astype(jnp.bfloat16)
-    low = (flux - high.astype(jnp.float32)).astype(jnp.bfloat16)
-    parts = jnp.concatenate([high, low, spots.astype(jnp.bfloat16)], axis=0)
-    placed = jnp.dot(parts, taken.astype(jnp.bfloat16), preferred_element_type=jnp.float32)
-    summed = placed[0:tr] + placed[tr : 2 * tr]
-    pieces = [summed[0:8], summed[8:16], placed[2 * tr : 2 * tr + 8]]
-    stacked = [
-        jnp.concatenate([piece[:, LANES * j : LANES * (j + 1)] for j in range(blocks)], axis=0)
-        for piece in pieces
-    ]
-    laneb = lax.broadcasted_iota(jnp.int32, (8 * blocks, LANES), 1)
-    for g in range(groups):
-        turned = [
-            pltpu.roll(s, (cap * (h - g)) % LANES, 1) if h != g else s
-            for h, s in enumerate(stacked)
-        ]
-        packed = jnp.where(laneb < cap, turned[0], jnp.where(laneb < 2 * cap, turned[1], turned[2]))
-        route_out[blocks * g : blocks * (g + 1)] = packed.reshape(blocks, 8, LANES)
-
-    @pl.loop(1, count)
-    def _(o):
-        route_copy(lax.rem(me + o, count), me).start()
-
-    route_in[place(me)] = route_out[place(me)]
 
     lon_copy(0).wait_recv()
     lon_copy(1).wait_recv()
@@ -290,9 +283,14 @@
             pltpu.roll(from_west, (LANES - 8 - 8 * p) % LANES, 1),
         )
 
-    for k in range(lev):
+    @pl.loop(0, lev)
+    def _(k):
         c = zon_ref[k]
-        ce = unpack(lon_in[1, lev], lon_in[0, lev], k, lane8)
+        ce = jnp.where(
+            lane8 < 8,
+            pltpu.roll(lon_in[0, lev], lax.rem(LANES - 8 * k, LANES), 1),
+            pltpu.roll(lon_in[1, lev], LANES - 8 - 8 * k, 1),
+        )
         before, before_e = ring(c, ce, -1, lane8)
         for m, weight in enumerate(cell_weights(c, before)):
             gz[k, m] = weight
@@ -333,14 +331,82 @@
             k = 2 * kp + parity
             for a in range(rows):
                 ext = unpack(from_west, from_east, parity * rows + a, lane)
-                zonal(k, a, column(k, a), ext)
+                zonal(k, a, st[k, WIDE + a], ext)
             send_rows(k)
 
     pair(0, (1,))
 
-    @pl.loop(1, lev // 2)
+    @pl.loop(1, lev // 4)
     def _(kp):
         pair(kp, (0, 1))
+
+    tile = tile_ref[...]
+    named = (tile == lax.broadcasted_iota(jnp.int32, (count, cells), 0)).astype(jnp.float32)
+    ahead = (
+        lax.broadcasted_iota(jnp.int32, (cells, cells), 0)
+        < lax.broadcasted_iota(jnp.int32, (cells, cells), 1)
+    ).astype(jnp.float32)
+    rank = jnp.dot(
+        named.astype(jnp.bfloat16), ahead.astype(jnp.bfloat16), preferred_element_type=jnp.float32
+    )
+    slot = jnp.sum(rank * named, axis=0, keepdims=True).astype(jnp.int32)
+    key = tile * cap + slot
+    spot = spot_ref[...]
+    spots = jnp.where(
+        lax.broadcasted_iota(jnp.int32, (16, cells), 0) == 0, spot // LANES, spot % LANES
+    ).astype(jnp.float32)
+    high = flux.astype(jnp.bfloat16)
+    low = (flux - high.astype(jnp.float32)).astype(jnp.bfloat16)
+    parts = jnp.concatenate([high, low, spots.astype(jnp.bfloat16)], axis=0)
+    lane_of = lax.broadcasted_iota(jnp.int32, (LANES, cells), 0)
+
+    @pl.loop(0, blocks)
+    def _(j):
+        taken = (key - j * LANES == lane_of).astype(jnp.float32).astype(jnp.bfloat16)
+        placed = lax.dot_general(
+            parts, taken, (((1,), (1,)), ((), ())), preferred_element_type=jnp.float32
+        )
+        summed = placed[0:tr] + placed[tr : 2 * tr]
+        slots[0, j] = summed[0:8]
+        slots[1, j] = summed[8:16]
+        slots[2, j] = placed[2 * tr : 2 * tr + 8]
+
+    stacked = [slots[h].reshape(8 * blocks, LANES) for h in range(3)]
+    laneb = lax.broadcasted_iota(jnp.int32, (8 * blocks, LANES), 1)
+    for g in range(groups):
+        turned = [
+            pltpu.roll(s, (cap * (h - g)) % LANES, 1) if h != g else s
+            for h, s in enumerate(stacked)
+        ]
+        packed = jnp.where(laneb < cap, turned[0], jnp.where(laneb < 2 * cap, turned[1], turned[2]))
+        route_out[blocks * g : blocks * (g + 1)] = packed.reshape(blocks, 8, LANES)
+
+    @pl.loop(1, count)
+    def _(o):
+        route_copy(lax.rem(me + o, count), me).start()
+
+    route_in[place(me)] = route_out[place(me)]
+
+    @pl.loop(lev // 4, lev // 2)
+    def _(kp):
+        pair(kp, (0, 1))
+
+    @pl.when(has_south)
+    def _():
+        mer_copy(1).wait_recv()
+
+    @pl.when(has_north)
+    def _():
+        mer_copy(0).wait_recv()
+
+    grid_row = lax.broadcasted_iota(jnp.int32, (3 * rows, LANES), 0) + (lat - 1) * rows
+    northern = (grid_row < n_lat * rows - 1).astype(jnp.float32)
+
+    @pl.loop(0, lev)
+    def _(k):
+        c = jnp.concatenate([mer_in[1, k], mer_ref[k], mer_in[0, k]], axis=0) * northern
+        for m, weight in enumerate(cell_weights(c, pltpu.roll(c, 1, 0))):
+            gm[k, m] = weight
 
     @pl.loop(1, count)
     def _(o):
@@ -375,7 +441,7 @@
     )
     emitted = emitted[: rows * tr] + emitted[rows * tr :]
 
-    surface = [column(0, a) + emitted[a * tr : (a + 1) * tr] for a in range(rows)]
+    surface = [st[0, WIDE + a] + emitted[a * tr : (a + 1) * tr] for a in range(rows)]
     left = jnp.zeros((tr, LANES), jnp.float32)
     right = left
     for a in range(rows):
@@ -388,66 +454,60 @@
     lon0_copy(0).start()
     lon0_copy(1).start()
 
-    @pl.when(has_south)
-    def _():
-        mer_copy(1).wait_recv()
-
-    @pl.when(has_north)
-    def _():
-        mer_copy(0).wait_recv()
-
-    grid_row = lax.broadcasted_iota(jnp.int32, (3 * rows, LANES), 0) + (lat - 1) * rows
-    northern = (grid_row < n_lat * rows - 1).astype(jnp.float32)
-
-    @pl.loop(0, lev)
-    def _(k):
-        c = jnp.concatenate([mer_in[1, k], mer_ref[k], mer_in[0, k]], axis=0) * northern
-        for m, weight in enumerate(cell_weights(c, pltpu.roll(c, 1, 0))):
-            gm[k, m] = weight
-
+    def meridional(k):
+        @pl.when(has_south)
+        def _():
+            lat_copy(k, 1).wait_recv()
+
+        @pl.when(has_north)
+        def _():
+            lat_copy(k, 0).wait_recv()
+
+        once = []
+        for a in range(-3, rows + 3):
+            new = 0.0
+            for m in range(7):
+                new = new + st[k, a + 3 + m] * gm[k, m, a + rows : a + rows + 1]
+            once.append(new)
+        for a in range(rows):
+            new = 0.0
+            for m in range(7):
+                new = new + once[a + m] * gm[k, m, a + rows : a + rows + 1]
+            fin[k, a] = new
+
+    def mixed(levels, opening, closing):
+        @pl.loop(0, rows)
+        def _(a):
+            part = [fin[j, a] for j in levels]
+            for k in range(lev):
+                total = 0.0 if opening else acc[a, k]
+                for j, value in zip(levels, part):
+                    total = total + value * mix_ref[a, k, j]
+                if closing:
+                    out_ref[pl.ds(k * rows + a, tr, stride=per), :] = total
+                else:
+                    acc[a, k] = total
+
+    cuts = [1, 1 + lev // 3, 1 + 2 * (lev // 3), lev]
+
+    def some(i):
+        @pl.loop(cuts[i], cuts[i + 1])
+        def _(k):
+            meridional(k)
+
+        mixed(range(cuts[i], cuts[i + 1]), i == 0, False)
+
+    load(11).wait()
+    some(0)
     lon0_copy(0).wait_recv()
     lon0_copy(1).wait_recv()
     for a in range(rows):
         zonal(0, a, fin[0, a], unpack(lon0_in[1], lon0_in[0], a, lane))
     send_rows(0)
-
-    def meridional(k):
-        @pl.when(has_south)
-        def _():
-            lat_copy(k, 1).wait_recv()
-
-        @pl.when(has_north)
-        def _():
-            lat_copy(k, 0).wait_recv()
-
-        for h in range(0, tr, 8):
-            once = []
-            for a in range(-3, rows + 3):
-                new = 0.0
-                for m in range(7):
-                    new = new + st[k, a + 3 + m, h : h + 8] * gm[k, m, a + rows : a + rows + 1]
-                once.append(new)
-            for a in range(rows):
-                new = 0.0
-                for m in range(7):
-                    new = new + once[a + m] * gm[k, m, a + rows : a + rows + 1]
-                fin[k, a, h : h + 8] = new
-
-    @pl.loop(1, lev)
-    def _(k):
-        meridional(k)
-
+    some(1)
+    some(2)
     meridional(0)
-
-    @pl.loop(0, rows)
-    def _(a):
-        for h in range(0, tr, 8):
-            held = [fin[j, a, h : h + 8] for j in range(lev)]
-            for k in range(lev):
-                total = held[0] * mix_ref[a, k, 0]
-                for j in range(1, lev):
-                    total = total + held[j] * mix_ref[a, k, j]
-                out_ref[pl.ds(h * per + k * rows + a, 8, stride=per), :] = total
+    mixed(range(1), False, True)
 
     for side in range(2):
         lon_copy(side).wait_send()
@@ -495,14 +555,29 @@
     count = n_lat * n_lon
     cap = 2 * cells // count
     f32 = jnp.float32
-    vmem = pl.BlockSpec(memory_space=pltpu.VMEM)
-    smem = pl.BlockSpec(memory_space=pltpu.SMEM)
+    args = (
+        features.T,
+        land_tile.T,
+        land_spot.reshape(1, -1),
+        w_in,
+        b_in.reshape(1, -1),
+        w_mid,
+        b_mid.reshape(1, -1),
+        w_out.T,
+        tracers.reshape(tr * lev * rows, cols),
+        zonal_wind,
+        meridional_wind,
+        mixing,
+    )
     out = pl.pallas_call(
         functools.partial(kernel, n_lat, n_lon, cap),
         out_shape=jax.ShapeDtypeStruct((tr * lev * rows, cols), f32),
-        in_specs=[vmem] * 11 + [smem],
-        out_specs=vmem,
-        scratch_shapes=[
+        in_specs=[pl.BlockSpec(memory_space=pltpu.HBM)] * len(args),
+        out_specs=pl.BlockSpec(memory_space=pltpu.VMEM),
+        scratch_shapes=[pltpu.VMEM(arg.shape, arg.dtype) for arg in args[:-1]]
+        + [
+            pltpu.SMEM(mixing.shape, f32),
+            pltpu.SemaphoreType.DMA((len(args),)),
             pltpu.VMEM((2, lev + 1, 8, cols), f32),
             pltpu.VMEM((2, lev + 1, 8, cols), f32),
             pltpu.VMEM((2, tr, cols), f32),
@@ -515,6 +590,8 @@
             pltpu.VMEM((lev, 7, 3 * rows, cols), f32),
             pltpu.VMEM((lev, rows + 2 * WIDE, tr, cols), f32),
             pltpu.VMEM((lev, rows, tr, cols), f32),
+            pltpu.VMEM((rows, lev, tr, cols), f32),
+            pltpu.VMEM((3, count * cap // cols, 8, cols), f32),
             pltpu.SemaphoreType.DMA((2, 2)),
             pltpu.SemaphoreType.DMA((2, 2)),
             pltpu.SemaphoreType.DMA((2, 2)),
@@ -524,22 +601,9 @@
             pltpu.SemaphoreType.DMA((2, lev)),
         ],
         compiler_params=pltpu.CompilerParams(
-            collective_id=0, has_side_effects=True, vmem_limit_bytes=40 * 1024 * 1024
+            collective_id=0, has_side_effects=True, vmem_limit_bytes=60 * 1024 * 1024
         ),
-    )(
-        features,
-        land_tile,
-        land_spot.reshape(1, -1),
-        w_in,
-        b_in.reshape(1, -1),
-        w_mid,
-        b_mid.reshape(1, -1),
-        w_out,
-        tracers.reshape(tr * lev * rows, cols),
-        zonal_wind,
-        meridional_wind,
-        mixing,
-    )
+    )(*args)
     return out.reshape(tr, lev, rows, cols)
 
 

time: 46.7 us -> 46.8 us (level)
  Pallas kernels: 41.8 us -> 44.3 us
  local copies, waits for them, and re-layouts: 4.6 us -> 2.3 us
    pallas_call x1, Pallas kernels: 41.8 us -> 44.3 us  [on_device(): pl.pallas_call(functools.partial(kernel, n_lat, n_lon, cap), out_shape=ja...]
    unnamed x26 -> x1, local copies, waits for them, and re-layouts: 4.6 us -> 2.3 us
where the time goes in v2:
time: 46.8 us; the launch traced here: 46.6 us
  Pallas kernels  44.3 us (95%)
  local copies, waits for them, and re-layouts  2.3 us (5%)
    pallas_call x1, Pallas kernels, on_device(): pl.pallas_call(functools.partial(kernel, n_lat, n_lon, cap), out_shape=ja...  44.3 us
    unnamed x1, local copies, waits for them, and re-layouts  2.3 us

profile of v2, /device:TPU:0, one launch (start us, length us, event | category | flops | bytes accessed | tf_op | source)
XLA Modules:
  0.0 46.6 jit_solution(9083713074094574076)
XLA Ops:
  0.0 44.3 %shard_map.118 = f32[2048,128]{1,0:T(8,128)} custom-call(bf16[64,512]{1,0:T(8,128)(2,1)} %bitcast.10, s32[1,512]{1,0:T(1,128)} %bitcast.12, s32[1,512]{1,0:T(1,128)} %bitcast.13, bf16[64,256]{1,0:T(8,128)(2,1)} %refs_3_.1, f32[1,256]{1,0:T(1,128)} %bitcast.14, bf16[256,256]{1,0:T(8,128)(2,1)} %refs_5_.1, f32[1,256]{1,0:T(1,128)} %bitcast.15, ...), custom_call_target="tpu_custom_call" | custom-call | tf_op jit(solution)/shard_map/pallas_call | solution.py:572
  44.3 2.3 %copy.14 = f32[16,16,8,128]{3,2,1,0:T(8,128)} copy(f32[16,16,8,128]{3,2,1,0:T(8,128)} %bitcast.8) | data formatting | bytes 2097152

commit v3 on v0

v3 whole, which is shorter than its diff:
```python
import functools

import jax
import jax.numpy as jnp
from jax import lax
from jax.experimental import pallas as pl
from jax.experimental.pallas import tpu as pltpu
from jax.sharding import PartitionSpec as P

MESH = pl.DeviceIdType.MESH
LANES = 128
WIDE = 6


def silu(v):
    return v / (1.0 + jnp.exp(-v))


def face_weights(c):
    p = jnp.maximum(c, 0.0)
    w = jnp.maximum(-c, 0.0)
    alpha = 0.5 * p * p
    beta = 1.0 - 2.0 / 3.0 * p
    gamma = 0.5 * w * w
    delta = 1.0 - 2.0 / 3.0 * w
    x = alpha * (1.0 - 3.0 * beta)
    y = c - alpha * (1.0 + 3.0 * beta) + gamma * (1.0 + 3.0 * delta)
    z = -gamma * (1.0 - 3.0 * delta)
    u = 6.0 * alpha * beta
    v = -6.0 * gamma * delta
    a, b = 7.0 / 12.0, 1.0 / 12.0
    return [
        -b * x,
        a * x - b * y,
        a * (x + y) - b * z + u,
        a * (y + z) - b * x + v,
        a * z - b * y,
        -b * z,
    ]


def cell_weights(c, before):
    f, g = face_weights(c), face_weights(before)
    out = [g[0]]
    for m in range(5):
        out.append(g[m + 1] - f[m])
    out.append(-f[5])
    out[3] = out[3] + 1.0
    return out


def route_kernel(
    n_lat,
    n_lon,
    cap,
    tr,
    rows,
    feat_ref,
    tile_ref,
    spot_ref,
    w_in_ref,
    b_in_ref,
    w_mid_ref,
    b_mid_ref,
    w_out_ref,
    out_ref,
    route_out,
    route_in,
    slots,
    route_send,
    route_recv,
):
    cells = feat_ref.shape[1]
    count = n_lat * n_lon
    groups = LANES // cap
    blocks = count // groups
    lat, lon = lax.axis_index("lat"), lax.axis_index("lon")
    me = lat * n_lon + lon

    def place(d):
        return lax.rem(d, groups) * blocks + d // groups

    barrier = pltpu.get_barrier_semaphore()

    @pl.loop(1, count)
    def _(o):
        d = lax.rem(me + o, count)
        pl.semaphore_signal(
            barrier, inc=1, device_id=(d // n_lon, lax.rem(d, n_lon)), device_id_type=MESH
        )

    first = silu(
        lax.dot_general(
            feat_ref[...], w_in_ref[...], (((0,), (0,)), ((), ())), preferred_element_type=jnp.float32
        )
        + b_in_ref[...]
    ).astype(jnp.bfloat16)
    second = silu(
        jnp.dot(first, w_mid_ref[...], preferred_element_type=jnp.float32) + b_mid_ref[...]
    ).astype(jnp.bfloat16)
    flux = lax.dot_general(
        w_out_ref[...], second, (((1,), (1,)), ((), ())), preferred_element_type=jnp.float32
    )

    tile = tile_ref[...]
    named = (tile == lax.broadcasted_iota(jnp.int32, (count, cells), 0)).astype(jnp.float32)
    ahead = (
        lax.broadcasted_iota(jnp.int32, (cells, cells), 0)
        < lax.broadcasted_iota(jnp.int32, (cells, cells), 1)
    ).astype(jnp.float32)
    rank = jnp.dot(
        named.astype(jnp.bfloat16), ahead.astype(jnp.bfloat16), preferred_element_type=jnp.float32
    )
    slot = jnp.sum(rank * named, axis=0, keepdims=True).astype(jnp.int32)
    key = tile * cap + slot
    spot = spot_ref[...]
    spots = jnp.where(
        lax.broadcasted_iota(jnp.int32, (16, cells), 0) == 0, spot // LANES, spot % LANES
    ).astype(jnp.float32)
    high = flux.astype(jnp.bfloat16)
    low = (flux - high.astype(jnp.float32)).astype(jnp.bfloat16)
    parts = jnp.concatenate([high, low, spots.astype(jnp.bfloat16)], axis=0)
    lane_of = lax.broadcasted_iota(jnp.int32, (LANES, cells), 0)

    @pl.loop(0, blocks)
    def _(j):
        taken = (key - j * LANES == lane_of).astype(jnp.float32).astype(jnp.bfloat16)
        placed = lax.dot_general(
            parts, taken, (((1,), (1,)), ((), ())), preferred_element_type=jnp.float32
        )
        summed = placed[0:tr] + placed[tr : 2 * tr]
        slots[0, j] = summed[0:8]
        slots[1, j] = summed[8:16]
        slots[2, j] = placed[2 * tr : 2 * tr + 8]

    stacked = [slots[h].reshape(8 * blocks, LANES) for h in range(3)]
    laneb = lax.broadcasted_iota(jnp.int32, (8 * blocks, LANES), 1)
    for g in range(groups):
        turned = [
            pltpu.roll(s, (cap * (h - g)) % LANES, 1) if h != g else s
            for h, s in enumerate(stacked)
        ]
        packed = jnp.where(laneb < cap, turned[0], jnp.where(laneb < 2 * cap, turned[1], turned[2]))
        route_out[blocks * g : blocks * (g + 1)] = packed.reshape(blocks, 8, LANES)

    pl.semaphore_wait(barrier, count - 1)

    def route_copy(d, origin):
        return pltpu.make_async_remote_copy(
            src_ref=route_out.at[place(d)],
            dst_ref=route_in.at[place(origin)],
            send_sem=route_send.at[d],
            recv_sem=route_recv.at[origin],
            device_id=(d // n_lon, lax.rem(d, n_lon)),
            device_id_type=MESH,
        )

    @pl.loop(1, count)
    def _(o):
        route_copy(lax.rem(me + o, count), me).start()

    route_in[place(me)] = route_out[place(me)]

    @pl.loop(1, count)
    def _(o):
        route_copy(me, lax.rem(me + o, count)).wait_recv()

    lists = [jnp.zeros((8 * blocks, LANES), jnp.float32)] * 3
    for g in range(groups):
        got = route_in[blocks * g : blocks * (g + 1)].reshape(8 * blocks, LANES)
        for h in range(3):
            turned = pltpu.roll(got, (cap * (g - h)) % LANES, 1) if g != h else got
            lists[h] = jnp.where(laneb // cap == g, turned, lists[h])
    entries = [
        jnp.concatenate([part[8 * j : 8 * (j + 1)] for j in range(blocks)], axis=1)
        for part in lists
    ]
    values = jnp.concatenate(entries[:2], axis=0)
    at_row, at_lane = entries[2][0:1], entries[2][1:2]
    wide = blocks * LANES
    onto = (
        lax.broadcasted_iota(jnp.int32, (LANES, wide), 0).astype(jnp.float32) == at_lane
    ).astype(jnp.float32)
    spread = jnp.concatenate(
        [jnp.where(at_row == float(a), values, 0.0) for a in range(rows)], axis=0
    )
    high = spread.astype(jnp.bfloat16)
    low = (spread - high.astype(jnp.float32)).astype(jnp.bfloat16)
    emitted = lax.dot_general(
        jnp.concatenate([high, low], axis=0),
        onto.astype(jnp.bfloat16),
        (((1,), (1,)), ((), ())),
        preferred_element_type=jnp.float32,
    )
    emitted = emitted[: rows * tr] + emitted[rows * tr :]

    out_ref[...] = emitted

    @pl.loop(1, count)
    def _(o):
        route_copy(lax.rem(me + o, count), me).wait_send()


def zonal_kernel(
    n_lon,
    x_ref,
    zon_ref,
    emitted_ref,
    st,
    lon_out,
    lon_in,
    gz,
    gze,
    held,
    lon_sem,
):
    lev, rows, _ = zon_ref.shape
    tr = st.shape[2]
    per = lev * rows
    lat, lon = lax.axis_index("lat"), lax.axis_index("lon")
    west, east = lax.rem(lon + n_lon - 1, n_lon), lax.rem(lon + 1, n_lon)
    barrier = pltpu.get_barrier_semaphore()
    for side in (west, east):
        pl.semaphore_signal(barrier, inc=1, device_id=(lat, side), device_id_type=MESH)

    lane = lax.broadcasted_iota(jnp.int32, (tr, LANES), 1)
    lane8 = lax.broadcasted_iota(jnp.int32, (rows, LANES), 1)

    def column(k, a):
        return x_ref[pl.ds(k * rows + a, tr, stride=per), :]

    @pl.loop(0, lev // 2)
    def _(kp):
        left = jnp.zeros((tr, LANES), jnp.float32)
        right = left
        for p in range(2 * rows):
            q = column(2 * kp + p // rows, p % rows)
            if p < rows:
                q = q + jnp.where(kp == 0, emitted_ref[p * tr : (p + 1) * tr], 0.0)
            held[2 * kp + p // rows, p % rows] = q
            mine = lane // 8 == p
            left = jnp.where(mine, pltpu.roll(q, 8 * p, 1), left)
            right = jnp.where(mine, pltpu.roll(q, (8 * p + 8) % LANES, 1), right)
        lon_out[0, pl.ds(2 * kp, 2)] = left.reshape(2, 8, LANES)
        lon_out[1, pl.ds(2 * kp, 2)] = right.reshape(2, 8, LANES)

    left = jnp.zeros((rows, LANES), jnp.float32)
    right = left
    for k in range(lev):
        c = zon_ref[k]
        mine = lane8 // 8 == k
        left = jnp.where(mine, pltpu.roll(c, (8 * k) % LANES, 1), left)
        right = jnp.where(mine, pltpu.roll(c, (8 * k + 8) % LANES, 1), right)
    lon_out[0, lev] = left
    lon_out[1, lev] = right

    pl.semaphore_wait(barrier, 2)

    def lon_copy(side):
        return pltpu.make_async_remote_copy(
            src_ref=lon_out.at[side],
            dst_ref=lon_in.at[side],
            send_sem=lon_sem.at[0, side],
            recv_sem=lon_sem.at[1, side],
            device_id=(lat, (west, east)[side]),
            device_id_type=MESH,
        )

    lon_copy(0).start()
    lon_copy(1).start()
    lon_copy(0).wait_recv()
    lon_copy(1).wait_recv()

    def ring(main, ext, m, where):
        if m == 0:
            return main, ext
        if m > 0:
            mask, turn = where < m, LANES - m
        else:
            mask, turn = where >= LANES + m, -m
        return (
            pltpu.roll(jnp.where(mask, ext, main), turn, 1),
            pltpu.roll(jnp.where(mask, main, ext), turn, 1),
        )

    def unpack(from_west, from_east, p, where):
        return jnp.where(
            where < 8,
            pltpu.roll(from_east, (LANES - 8 * p) % LANES, 1),
            pltpu.roll(from_west, (LANES - 8 - 8 * p) % LANES, 1),
        )

    @pl.loop(0, lev)
    def _(k):
        c = zon_ref[k]
        ce = jnp.where(
            lane8 < 8,
            pltpu.roll(lon_in[0, lev], lax.rem(LANES - 8 * k, LANES), 1),
            pltpu.roll(lon_in[1, lev], LANES - 8 - 8 * k, 1),
        )
        before, before_e = ring(c, ce, -1, lane8)
        for m, weight in enumerate(cell_weights(c, before)):
            gz[k, m] = weight
        for m, weight in enumerate(cell_weights(ce, before_e)):
            gze[k, m] = weight

    def zonal(k, a, main, ext):
        new, new_e = 0.0, 0.0
        for m in range(-3, 4):
            near, near_e = ring(main, ext, m, lane)
            new = new + near * gz[k, m + 3, a : a + 1, :]
            new_e = new_e + near_e * gze[k, m + 3, a : a + 1, :]
        main, ext = new, new_e
        new = 0.0
        for m in range(-3, 4):
            if m == 0:
                near = main
            elif m > 0:
                near = pltpu.roll(jnp.where(lane < m, ext, main), LANES - m, 1)
            else:
                near = pltpu.roll(jnp.where(lane >= LANES + m, ext, main), -m, 1)
            new = new + near * gz[k, m + 3, a : a + 1, :]
        st[k, a] = new

    def pair(kp, parities):
        from_west = lon_in[1, pl.ds(2 * kp, 2)].reshape(tr, LANES)
        from_east = lon_in[0, pl.ds(2 * kp, 2)].reshape(tr, LANES)
        for parity in parities:
            k = 2 * kp + parity
            for a in range(rows):
                ext = unpack(from_west, from_east, parity * rows + a, lane)
                zonal(k, a, held[k, a], ext)

    @pl.loop(0, lev // 2)
    def _(kp):
        pair(kp, (0, 1))

    lon_copy(0).wait_send()
    lon_copy(1).wait_send()


def meridional_kernel(
    n_lat,
    st,
    mer_ref,
    fin,
    mer_in,
    halo,
    gm,
    mer_sem,
    lat_send,
    lat_recv,
):
    lev, rows, tr, _ = st.shape
    lat, lon = lax.axis_index("lat"), lax.axis_index("lon")
    has_south, has_north = lat > 0, lat < n_lat - 1
    barrier = pltpu.get_barrier_semaphore()

    @pl.when(has_south)
    def _():
        pl.semaphore_signal(barrier, inc=1, device_id=(lat - 1, lon), device_id_type=MESH)

    @pl.when(has_north)
    def _():
        pl.semaphore_signal(barrier, inc=1, device_id=(lat + 1, lon), device_id_type=MESH)

    between = jnp.logical_and(has_south, has_north)

    @pl.when(between)
    def _():
        pl.semaphore_wait(barrier, 2)

    @pl.when(jnp.logical_not(between))
    def _():
        pl.semaphore_wait(barrier, 1)

    def mer_copy(side):
        return pltpu.make_async_remote_copy(
            src_ref=mer_ref,
            dst_ref=mer_in.at[side],
            send_sem=mer_sem.at[0, side],
            recv_sem=mer_sem.at[1, side],
            device_id=(lat + (-1, 1)[side], lon),
            device_id_type=MESH,
        )

    def lat_copy(k, side):
        return pltpu.make_async_remote_copy(
            src_ref=st.at[k, pl.ds((0, rows - WIDE)[side], WIDE)],
            dst_ref=halo.at[side, k],
            send_sem=lat_send.at[side, k],
            recv_sem=lat_recv.at[side, k],
            device_id=(lat + (-1, 1)[side], lon),
            device_id_type=MESH,
        )

    @pl.when(has_south)
    def _():
        mer_copy(0).start()

    @pl.when(has_north)
    def _():
        mer_copy(1).start()

    @pl.loop(0, lev)
    def _(k):
        @pl.when(has_south)
        def _():
            lat_copy(k, 0).start()

        @pl.when(has_north)
        def _():
            lat_copy(k, 1).start()

    @pl.when(jnp.logical_not(has_south))
    def _():
        mer_in[1] = jnp.zeros((lev, rows, LANES), jnp.float32)

        @pl.loop(0, lev)
        def _(k):
            halo[1, k] = jnp.zeros((WIDE, tr, LANES), jnp.float32)

    @pl.when(jnp.logical_not(has_north))
    def _():
        mer_in[0] = jnp.zeros((lev, rows, LANES), jnp.float32)

        @pl.loop(0, lev)
        def _(k):
            halo[0, k] = jnp.zeros((WIDE, tr, LANES), jnp.float32)

    @pl.when(has_south)
    def _():
        mer_copy(1).wait_recv()

    @pl.when(has_north)
    def _():
        mer_copy(0).wait_recv()

    grid_row = lax.broadcasted_iota(jnp.int32, (3 * rows, LANES), 0) + (lat - 1) * rows
    northern = (grid_row < n_lat * rows - 1).astype(jnp.float32)

    @pl.loop(0, lev)
    def _(k):
        c = jnp.concatenate([mer_in[1, k], mer_ref[k], mer_in[0, k]], axis=0) * northern
        for m, weight in enumerate(cell_weights(c, pltpu.roll(c, 1, 0))):
            gm[k, m] = weight

    def meridional(k):
        @pl.when(has_south)
        def _():
            lat_copy(k, 1).wait_recv()

        @pl.when(has_north)
        def _():
            lat_copy(k, 0).wait_recv()

        whole = (
            [halo[1, k, a] for a in range(WIDE)]
            + [st[k, a] for a in range(rows)]
            + [halo[0, k, a] for a in range(WIDE)]
        )
        once = []
        for a in range(-3, rows + 3):
            new = 0.0
            for m in range(7):
                new = new + whole[a + 3 + m] * gm[k, m, a + rows : a + rows + 1]
            once.append(new)
        for a in range(rows):
            new = 0.0
            for m in range(7):
                new = new + once[a + m] * gm[k, m, a + rows : a + rows + 1]
            fin[k, a] = new

    @pl.loop(0, lev)
    def _(k):
        meridional(k)

    @pl.when(has_south)
    def _():
        mer_copy(0).wait_send()

        @pl.loop(0, lev)
        def _(k):
            lat_copy(k, 0).wait_send()

    @pl.when(has_north)
    def _():
        mer_copy(1).wait_send()

        @pl.loop(0, lev)
        def _(k):
            lat_copy(k, 1).wait_send()


def mixing_kernel(fin, mix_ref, out_ref):
    lev, rows, tr, _ = fin.shape
    per = lev * rows

    @pl.loop(0, rows)
    def _(a):
        part = [fin[j, a] for j in range(lev)]
        for k in range(lev):
            total = part[0] * mix_ref[a, k, 0]
            for j in range(1, lev):
                total = total + part[j] * mix_ref[a, k, j]
            out_ref[pl.ds(k * rows + a, tr, stride=per), :] = total


def on_device(
    n_lat,
    n_lon,
    features,
    land_tile,
    land_spot,
    w_in,
    b_in,
    w_mid,
    b_mid,
    w_out,
    tracers,
    zonal_wind,
    meridional_wind,
    mixing,
):
    tr, lev, rows, cols = tracers.shape
    cells = features.shape[0]
    count = n_lat * n_lon
    cap = 2 * cells // count
    f32 = jnp.float32
    vmem = pl.BlockSpec(memory_space=pltpu.VMEM)
    smem = pl.BlockSpec(memory_space=pltpu.SMEM)
    dma = pltpu.SemaphoreType.DMA

    def params(number):
        return pltpu.CompilerParams(
            collective_id=number, has_side_effects=True, vmem_limit_bytes=16 * 1024 * 1024
        )

    emitted = pl.pallas_call(
        functools.partial(route_kernel, n_lat, n_lon, cap, tr, rows),
        out_shape=jax.ShapeDtypeStruct((rows * tr, cols), f32),
        in_specs=[vmem] * 8,
        out_specs=vmem,
        scratch_shapes=[
            pltpu.VMEM((count, 8, cols), f32),
            pltpu.VMEM((count, 8, cols), f32),
            pltpu.VMEM((3, count * cap // cols, 8, cols), f32),
            dma((count,)),
            dma((count,)),
        ],
        compiler_params=params(0),
    )(
        features.T,
        land_tile.T,
        land_spot.reshape(1, -1),
        w_in,
        b_in.reshape(1, -1),
        w_mid,
        b_mid.reshape(1, -1),
        w_out.T,
    )
    blown = pl.pallas_call(
        functools.partial(zonal_kernel, n_lon),
        out_shape=jax.ShapeDtypeStruct((lev, rows, tr, cols), f32),
        in_specs=[vmem] * 3,
        out_specs=vmem,
        scratch_shapes=[
            pltpu.VMEM((2, lev + 1, 8, cols), f32),
            pltpu.VMEM((2, lev + 1, 8, cols), f32),
            pltpu.VMEM((lev, 7, rows, cols), f32),
            pltpu.VMEM((lev, 7, rows, cols), f32),
            pltpu.VMEM((lev, rows, tr, cols), f32),
            dma((2, 2)),
        ],
        compiler_params=params(1),
    )(tracers.reshape(tr * lev * rows, cols), zonal_wind, emitted)
    swept = pl.pallas_call(
        functools.partial(meridional_kernel, n_lat),
        out_shape=jax.ShapeDtypeStruct((lev, rows, tr, cols), f32),
        in_specs=[vmem] * 2,
        out_specs=vmem,
        scratch_shapes=[
            pltpu.VMEM((2, lev, rows, cols), f32),
            pltpu.VMEM((2, lev, WIDE, tr, cols), f32),
            pltpu.VMEM((lev, 7, 3 * rows, cols), f32),
            dma((2, 2)),
            dma((2, lev)),
            dma((2, lev)),
        ],
        compiler_params=params(2),
    )(blown, meridional_wind)
    out = pl.pallas_call(
        mixing_kernel,
        out_shape=jax.ShapeDtypeStruct((tr * lev * rows, cols), f32),
        in_specs=[vmem, smem],
        out_specs=vmem,
        compiler_params=pltpu.CompilerParams(vmem_limit_bytes=16 * 1024 * 1024),
    )(swept, mixing)
    return out.reshape(tr, lev, rows, cols)


def solution(mesh):
    placed = (
        P(("lat", "lon"), None),
        P(("lat", "lon"), None),
        P(("lat", "lon")),
        P(),
        P(),
        P(),
        P(),
        P(),
        P(None, None, "lat", "lon"),
        P(None, "lat", "lon"),
        P(None, "lat", "lon"),
        P("lat", None, None),
    )
    return jax.shard_map(
        functools.partial(on_device, mesh.shape["lat"], mesh.shape["lon"]),
        mesh=mesh,
        in_specs=placed,
        out_specs=P(None, None, "lat", "lon"),
        check_vma=False,
    )
```

time: 205 us -> 70.5 us (0.34)
  local copies, waits for them, and re-layouts: 112 us -> 5.14 us
  Pallas kernels: 0 us -> 65 us
  waiting for transfers between devices: 30.6 us -> 0 us
  other arithmetic: 30.1 us -> 0 us
  starting transfers between devices: 27.4 us -> 0 us
    scatter x3 -> x0, local copies, waits for them, and re-layouts: 91 us -> none  [the longest x1 66.6 us: on_device(): places = jnp.zeros((device_count, capacity), jnp.float32).at[owner_tile,...]
    pallas_call x0 -> x4, Pallas kernels: none -> 65 us  [the longest x1 26.9 us: on_device(): pl.pallas_call(functools.partial(zonal_kernel, n_lon), out_shape=jax.Shap...]
    ppermute x8 -> x0, waiting for transfers between devices: 23.3 us -> none  [the longest x4 14.9 us: with_halo(): lax.ppermute(lax.slice_in_dim(block, block.shape[dim] - width, None, axis...]
    all_to_all x2 -> x0, starting transfers between devices: 13.7 us -> none  [the longest x1 7.86 us: on_device(): lax.all_to_all(places, ('lat', 'lon'), split_axis=0, concat_axis=0, tiled...]
    ppermute x8 -> x0, starting transfers between devices: 13.7 us -> none  [the longest x4 8.6 us: with_halo(): lax.ppermute(lax.slice_in_dim(block, 0, width, axis=dim), axis, backward)]
    all_to_all x2 -> x0, waiting for transfers between devices: 7.26 us -> none  [the longest x1 7.26 us: on_device(): lax.all_to_all(outgoing, ('lat', 'lon'), split_axis=0, concat_axis=0, til...]
    ppermute x4 -> x0, local copies, waits for them, and re-layouts: 6.94 us -> none  [the longest x2 4.41 us: with_halo(): lax.ppermute(lax.slice_in_dim(block, 0, width, axis=dim), axis, backward)]
    sub x11 -> x0, other arithmetic: 6.79 us -> none  [the longest x4 3.06 us: transport(): 7.0 / 12.0 * (section(values, 1, -2, axis) + section(values, 2, -1, axis))]
  transfers between devices with their start and end apart: 10 -> 0, of which waited for: 7 -> 0; matrix products, arithmetic and copies ran while one was open for 17% -> 0% of each run, Pallas kernels for 0% -> 0%
where the time goes in v3:
time: 70.5 us; the launch traced here: 70.2 us
  Pallas kernels  65 us (92%)
  local copies, waits for them, and re-layouts  5.14 us (7%)
    pallas_call x1, Pallas kernels, on_device(): pl.pallas_call(functools.partial(zonal_kernel, n_lon), out_shape=jax.Shap...  26.9 us
    pallas_call x1, Pallas kernels, on_device(): pl.pallas_call(functools.partial(meridional_kernel, n_lat), out_shape=jax...  21.6 us
    pallas_call x1, Pallas kernels, on_device(): pl.pallas_call(functools.partial(route_kernel, n_lat, n_lon, cap, tr, row...  12.4 us
    unnamed x24, local copies, waits for them, and re-layouts  5.14 us
    pallas_call x1, Pallas kernels, on_device(): pl.pallas_call(mixing_kernel, out_shape=jax.ShapeDtypeStruct((tr * lev *...  4.17 us

profile of v3, /device:TPU:0, one launch (start us, length us, event | category | flops | bytes accessed | tf_op | source)
XLA Modules:
  0.0 70.2 jit_solution(2707677568747909931)
XLA Ops:
  0.0 0.0 copy-start.7
  0.0 0.0 copy-start.9
  0.0 0.0 copy-start.8
  0.0 0.0 copy-start.10
  0.0 0.7 copy-done.7
  0.7 0.0 copy-done.9
  0.7 0.0 copy-done.8
  0.7 0.0 copy-done.10
  0.7 0.0 copy-start.1
  0.7 0.9 %copy-done.1 = bf16[256,256]{1,0:T(8,128)(2,1)S(1)} copy-done((bf16[256,256]{1,0:T(8,128)(2,1)S(1)}, bf16[256,256]{1,0:T(8,128)(2,1)}, u32[]{:S(2)}) %copy-start.1) | copy-done | bytes 131096
  1.6 0.0 copy-start.2
  1.6 0.8 %copy-done.2 = bf16[512,64]{0,1:T(8,128)(2,1)S(1)} copy-done((bf16[512,64]{0,1:T(8,128)(2,1)S(1)}, bf16[512,64]{0,1:T(8,128)(2,1)}, u32[]{:S(2)}) %copy-start.2) | copy-done | bytes 65560
  2.5 0.0 copy-start.6
  2.5 0.8 %copy-done.6 = bf16[64,256]{1,0:T(8,128)(2,1)S(1)} copy-done((bf16[64,256]{1,0:T(8,128)(2,1)S(1)}, bf16[64,256]{1,0:T(8,128)(2,1)}, u32[]{:S(2)}) %copy-start.6) | copy-done | bytes 32792
  3.2 0.0 copy-start.11
  3.2 0.7 copy-done.11
  3.9 0.0 copy-start.3
  3.9 12.4 %shard_map.118.emitted_ref = f32[128,128]{1,0:T(8,128)S(1)} custom-call(bf16[64,512]{1,0:T(8,128)(2,1)S(1)} %bitcast.9, s32[1,512]{1,0:T(1,128)S(1)} %bitcast.11, s32[1,512]{1,0:T(1,128)S(1)} %bitcast.12, bf16[64,256]{1,0:T(8,128)(2,1)S(1)} %copy-done.6, f32[1,256]{1,0:T(1,128)S(1)} %bitcast.13, bf16[256,256]{1,0:T(8,128)(2,1)S(1)} %copy-done.1, ...), custom_call_target="tpu_custom_call" | custom-call | tf_op jit(solution)/shard_map/pallas_call | solution.py:539
  16.3 0.0 copy-done.3
  16.3 0.0 copy-start
  16.3 1.2 %copy-done = f32[16,16,8,128]{3,2,1,0:T(8,128)S(1)} copy-done((f32[16,16,8,128]{3,2,1,0:T(8,128)S(1)}, f32[16,16,8,128]{3,2,1,0:T(8,128)}, u32[]{:S(2)}) %copy-start) | copy-done | bytes 1048600
  17.5 0.0 copy-start.4
  17.5 26.9 %shard_map.119.st = f32[16,8,16,128]{3,2,1,0:T(8,128)S(1)} custom-call(f32[2048,128]{1,0:T(8,128)S(1)} %bitcast.8, f32[16,8,128]{2,1,0:T(8,128)S(1)} %copy-done.3, f32[128,128]{1,0:T(8,128)S(1)} %shard_map.118.emitted_ref), custom_call_target="tpu_custom_call" | custom-call | tf_op jit(solution)/shard_map/pallas_call | solution.py:562
  44.4 0.0 copy-done.4
  44.4 0.0 copy-start.5
  44.4 21.6 %shard_map.120.fin = f32[16,8,16,128]{3,2,1,0:T(8,128)S(1)} custom-call(f32[16,8,16,128]{3,2,1,0:T(8,128)S(1)} %shard_map.119.st, f32[16,8,128]{2,1,0:T(8,128)S(1)} %copy-done.4), custom_call_target="tpu_custom_call" | custom-call | tf_op jit(solution)/shard_map/pallas_call | solution.py:577
  66.0 0.0 copy-done.5
  66.0 4.2 %shard_map.121 = f32[2048,128]{1,0:T(8,128)} custom-call(f32[16,8,16,128]{3,2,1,0:T(8,128)S(1)} %shard_map.120.fin, f32[8,16,16]{2,1,0:T(8,128)S(1)} %copy-done.5), custom_call_target="tpu_custom_call" | custom-call | tf_op jit(solution)/shard_map/pallas_call | solution.py:592
Async XLA Ops:
  0.0 0.7 copy-start.7
  0.0 0.7 copy-start.9
  0.0 0.7 %copy-start.8 = (s32[512,1]{0,1:T(1,128)S(1)}, s32[512,1]{0,1:T(1,128)}, u32[]{:S(2)}) copy-start(s32[512,1]{0,1:T(1,128)} %param.13) | copy-start | bytes 6148
  0.0 0.7 %copy-start.10 = (f32[256]{0:T(256)S(1)}, f32[256]{0:T(256)}, u32[]{:S(2)}) copy-start(f32[256]{0:T(256)} %param.16) | copy-start | bytes 3076
  0.7 0.9 %copy-start.1 = (bf16[256,256]{1,0:T(8,128)(2,1)S(1)}, bf16[256,256]{1,0:T(8,128)(2,1)}, u32[]{:S(2)}) copy-start(bf16[256,256]{1,0:T(8,128)(2,1)} %w_mid_ref.1) | copy-start | bytes 393220
  1.6 0.8 %copy-start.2 = (bf16[512,64]{0,1:T(8,128)(2,1)S(1)}, bf16[512,64]{0,1:T(8,128)(2,1)}, u32[]{:S(2)}) copy-start(bf16[512,64]{0,1:T(8,128)(2,1)} %param.12) | copy-start | bytes 196612
  2.5 0.8 %copy-start.6 = (bf16[64,256]{1,0:T(8,128)(2,1)S(1)}, bf16[64,256]{1,0:T(8,128)(2,1)}, u32[]{:S(2)}) copy-start(bf16[64,256]{1,0:T(8,128)(2,1)} %w_in_ref.1) | copy-start | bytes 98308
  3.2 0.7 copy-start.11
  3.9 12.4 %copy-start.3 = (f32[16,8,128]{2,1,0:T(8,128)S(1)}, f32[16,8,128]{2,1,0:T(8,128)}, u32[]{:S(2)}) copy-start(f32[16,8,128]{2,1,0:T(8,128)} %zon_ref.1) | copy-start | bytes 196612
  16.3 1.2 %copy-start = (f32[16,16,8,128]{3,2,1,0:T(8,128)S(1)}, f32[16,16,8,128]{3,2,1,0:T(8,128)}, u32[]{:S(2)}) copy-start(f32[16,16,8,128]{3,2,1,0:T(8,128)} %param.20) | copy-start | bytes 3145732
  17.5 26.9 %copy-start.4 = (f32[16,8,128]{2,1,0:T(8,128)S(1)}, f32[16,8,128]{2,1,0:T(8,128)}, u32[]{:S(2)}) copy-start(f32[16,8,128]{2,1,0:T(8,128)} %mer_ref.1) | copy-start | bytes 196612
  44.4 21.6 %copy-start.5 = (f32[8,16,16]{2,1,0:T(8,128)S(1)}, f32[8,16,16]{2,1,0:T(8,128)}, u32[]{:S(2)}) copy-start(f32[8,16,16]{2,1,0:T(8,128)} %mix_ref.1) | copy-start | bytes 24580

commit v4 on v2

--- a/solution.py
+++ b/solution.py
@@ -68,15 +68,14 @@
     held,
     out_ref,
     given_sem,
-    lon_out,
-    lon_in,
-    lon0_out,
-    lon0_in,
+    zb,
+    once_z,
+    twice_z,
+    wz,
+    wk,
     mer_in,
     route_out,
     route_in,
-    gz,
-    gze,
     gm,
     st,
     fin,
@@ -134,12 +133,6 @@
             barrier, inc=1, device_id=(d // n_lon, lax.rem(d, n_lon)), device_id_type=MESH
         )
 
-    lane = lax.broadcasted_iota(jnp.int32, (tr, LANES), 1)
-    lane8 = lax.broadcasted_iota(jnp.int32, (rows, LANES), 1)
-
-    def column(k, a):
-        return x_ref[pl.ds(k * rows + a, tr, stride=per), :]
-
     @pl.when(jnp.logical_not(has_south))
     def _():
         mer_in[1] = jnp.zeros((lev, rows, LANES), jnp.float32)
@@ -158,36 +151,35 @@
 
     load(8).wait()
 
-    @pl.loop(0, lev // 2)
-    def _(kp):
-        left = jnp.zeros((tr, LANES), jnp.float32)
-        right = left
-        for p in range(2 * rows):
-            q = column(2 * kp + p // rows, p % rows)
-            st[2 * kp + p // rows, WIDE + p % rows] = q
-            mine = lane // 8 == p
-            left = jnp.where(mine, pltpu.roll(q, 8 * p, 1), left)
-            right = jnp.where(mine, pltpu.roll(q, (8 * p + 8) % LANES, 1), right)
-        lon_out[0, pl.ds(2 * kp, 2)] = left.reshape(2, 8, LANES)
-        lon_out[1, pl.ds(2 * kp, 2)] = right.reshape(2, 8, LANES)
+    def halves(v):
+        high = v.astype(jnp.bfloat16)
+        low = (v - high.astype(jnp.float32)).astype(jnp.bfloat16)
+        return jnp.concatenate([high, low], axis=1)
+
+    def turned_by(order, v):
+        return lax.dot_general(
+            order, halves(v), (((1,), (1,)), ((), ())), preferred_element_type=jnp.float32
+        )
+
+    cell = lax.broadcasted_iota(jnp.int32, (LANES, 2 * LANES), 0)
+    from_cell = lax.broadcasted_iota(jnp.int32, (LANES, 2 * LANES), 1) % LANES
+    straight = (cell == from_cell).astype(jnp.float32).astype(jnp.bfloat16)
+    by_row = (cell % tr * rows + cell // tr == from_cell).astype(jnp.float32).astype(jnp.bfloat16)
+    own = slice(16, 16 + LANES)
+
+    @pl.loop(1, lev)
+    def _(k):
+        zb[k, own] = turned_by(straight, x_ref[:, k].reshape(tr * rows, LANES))
 
     load(9).wait()
-    left = jnp.zeros((rows, LANES), jnp.float32)
-    right = left
-    for k in range(lev):
-        c = zon_ref[k]
-        mine = lane8 // 8 == k
-        left = jnp.where(mine, pltpu.roll(c, (8 * k) % LANES, 1), left)
-        right = jnp.where(mine, pltpu.roll(c, (8 * k + 8) % LANES, 1), right)
-    lon_out[0, lev] = left
-    lon_out[1, lev] = right
+    zb[lev, own] = turned_by(straight, zon_ref[...].reshape(lev * rows, LANES))
 
     pl.semaphore_wait(barrier, count - 1)
 
     def lon_copy(side):
         return pltpu.make_async_remote_copy(
-            src_ref=lon_out.at[side],
-            dst_ref=lon_in.at[side],
+            src_ref=zb.at[pl.ds(1, lev), pl.ds((16, 8 + LANES)[side], 8)],
+            dst_ref=zb.at[pl.ds(1, lev), pl.ds((16 + LANES, 8)[side], 8)],
             send_sem=lon_sem.at[0, side],
             recv_sem=lon_sem.at[1, side],
             device_id=(lat, (west, east)[side]),
@@ -196,8 +188,8 @@
 
     def lon0_copy(side):
         return pltpu.make_async_remote_copy(
-            src_ref=lon0_out.at[side],
-            dst_ref=lon0_in.at[side],
+            src_ref=zb.at[0, pl.ds((16, 8 + LANES)[side], 8)],
+            dst_ref=zb.at[0, pl.ds((16 + LANES, 8)[side], 8)],
             send_sem=lon0_sem.at[0, side],
             recv_sem=lon0_sem.at[1, side],
             device_id=(lat, (west, east)[side]),
@@ -264,56 +256,45 @@
     lon_copy(0).wait_recv()
     lon_copy(1).wait_recv()
 
-    def ring(main, ext, m, where):
-        if m == 0:
-            return main, ext
-        if m > 0:
-            mask, turn = where < m, LANES - m
-        else:
-            mask, turn = where >= LANES + m, -m
-        return (
-            pltpu.roll(jnp.where(mask, ext, main), turn, 1),
-            pltpu.roll(jnp.where(mask, main, ext), turn, 1),
-        )
-
-    def unpack(from_west, from_east, p, where):
-        return jnp.where(
-            where < 8,
-            pltpu.roll(from_east, (LANES - 8 * p) % LANES, 1),
-            pltpu.roll(from_west, (LANES - 8 - 8 * p) % LANES, 1),
-        )
-
-    @pl.loop(0, lev)
-    def _(k):
-        c = zon_ref[k]
-        ce = jnp.where(
-            lane8 < 8,
-            pltpu.roll(lon_in[0, lev], lax.rem(LANES - 8 * k, LANES), 1),
-            pltpu.roll(lon_in[1, lev], LANES - 8 - 8 * k, 1),
-        )
-        before, before_e = ring(c, ce, -1, lane8)
-        for m, weight in enumerate(cell_weights(c, before)):
-            gz[k, m] = weight
-        for m, weight in enumerate(cell_weights(ce, before_e)):
-            gze[k, m] = weight
-
-    def zonal(k, a, main, ext):
-        new, new_e = 0.0, 0.0
-        for m in range(-3, 4):
-            near, near_e = ring(main, ext, m, lane)
-            new = new + near * gz[k, m + 3, a : a + 1, :]
-            new_e = new_e + near_e * gze[k, m + 3, a : a + 1, :]
-        main, ext = new, new_e
-        new = 0.0
-        for m in range(-3, 4):
-            if m == 0:
-                near = main
-            elif m > 0:
-                near = pltpu.roll(jnp.where(lane < m, ext, main), LANES - m, 1)
-            else:
-                near = pltpu.roll(jnp.where(lane >= LANES + m, ext, main), -m, 1)
-            new = new + near * gz[k, m + 3, a : a + 1, :]
-        st[k, WIDE + a] = new
+    wide_cols = LANES + 16
+    c = zb[lev, 8 : 8 + wide_cols]
+    before = zb[lev, 7 : 7 + wide_cols]
+    for m, weight in enumerate(cell_weights(c, before)):
+        wz[m * wide_cols : (m + 1) * wide_cols] = halves(weight)
+    pick_from = lax.broadcasted_iota(jnp.int32, (2 * LANES, LANES), 0) % LANES
+    pick_row = lax.broadcasted_iota(jnp.int32, (2 * LANES, LANES), 1) % rows
+
+    def zonal(k):
+        pick = (pick_from == pick_row + k * rows).astype(jnp.float32).astype(jnp.bfloat16)
+        for m in range(7):
+            wk[m * wide_cols : (m + 1) * wide_cols] = jnp.dot(
+                wz[m * wide_cols : (m + 1) * wide_cols], pick, preferred_element_type=jnp.float32
+            )
+        third = wide_cols // 3
+
+        @pl.loop(0, 3)
+        def _(i):
+            new = 0.0
+            for m in range(7):
+                new = new + (
+                    zb[k, pl.ds(i * third + 5 + m, third)]
+                    * wk[pl.ds(pl.multiple_of(i * third + m * wide_cols, 8), third)]
+                )
+            once_z[pl.ds(pl.multiple_of(i * third + 8, 8), third)] = new
+
+        half = LANES // 2
+
+        @pl.loop(0, 2)
+        def _(i):
+            new = 0.0
+            for m in range(7):
+                new = new + (
+                    once_z[pl.ds(i * half + 13 + m, half)]
+                    * wk[pl.ds(pl.multiple_of(i * half + 8 + m * wide_cols, 8), half)]
+                )
+            twice_z[pl.ds(pl.multiple_of(i * half, 8), half)] = new
+
+        st[k, WIDE : WIDE + rows] = turned_by(by_row, twice_z[...]).reshape(rows, tr, LANES)
 
     def send_rows(k):
         @pl.when(has_south)
@@ -324,21 +305,10 @@
         def _():
             lat_copy(k, 1).start()
 
-    def pair(kp, parities):
-        from_west = lon_in[1, pl.ds(2 * kp, 2)].reshape(tr, LANES)
-        from_east = lon_in[0, pl.ds(2 * kp, 2)].reshape(tr, LANES)
-        for parity in parities:
-            k = 2 * kp + parity
-            for a in range(rows):
-                ext = unpack(from_west, from_east, parity * rows + a, lane)
-                zonal(k, a, st[k, WIDE + a], ext)
-            send_rows(k)
-
-    pair(0, (1,))
-
-    @pl.loop(1, lev // 4)
-    def _(kp):
-        pair(kp, (0, 1))
+    @pl.loop(1, lev // 2)
+    def _(k):
+        zonal(k)
+        send_rows(k)
 
     tile = tile_ref[...]
     named = (tile == lax.broadcasted_iota(jnp.int32, (count, cells), 0)).astype(jnp.float32)
@@ -387,9 +357,10 @@
 
     route_in[place(me)] = route_out[place(me)]
 
-    @pl.loop(lev // 4, lev // 2)
-    def _(kp):
-        pair(kp, (0, 1))
+    @pl.loop(lev // 2, lev)
+    def _(k):
+        zonal(k)
+        send_rows(k)
 
     @pl.when(has_south)
     def _():
@@ -428,8 +399,9 @@
     onto = (
         lax.broadcasted_iota(jnp.int32, (LANES, wide), 0).astype(jnp.float32) == at_lane
     ).astype(jnp.float32)
+    row_of = lax.broadcasted_iota(jnp.int32, (rows, wide), 0).astype(jnp.float32)
     spread = jnp.concatenate(
-        [jnp.where(at_row == float(a), values, 0.0) for a in range(rows)], axis=0
+        [jnp.where(at_row == row_of, values[t : t + 1], 0.0) for t in range(tr)], axis=0
     )
     high = spread.astype(jnp.bfloat16)
     low = (spread - high.astype(jnp.float32)).astype(jnp.bfloat16)
@@ -441,16 +413,8 @@
     )
     emitted = emitted[: rows * tr] + emitted[rows * tr :]
 
-    surface = [st[0, WIDE + a] + emitted[a * tr : (a + 1) * tr] for a in range(rows)]
-    left = jnp.zeros((tr, LANES), jnp.float32)
-    right = left
-    for a in range(rows):
-        mine = lane // 8 == a
-        left = jnp.where(mine, pltpu.roll(surface[a], 8 * a, 1), left)
-        right = jnp.where(mine, pltpu.roll(surface[a], 8 * a + 8, 1), right)
-        fin[0, a] = surface[a]
-    lon0_out[0] = left
-    lon0_out[1] = right
+    surface = x_ref[:, 0].reshape(tr * rows, LANES) + emitted
+    zb[0, own] = turned_by(straight, surface)
     lon0_copy(0).start()
     lon0_copy(1).start()
 
@@ -501,8 +465,7 @@
     some(0)
     lon0_copy(0).wait_recv()
     lon0_copy(1).wait_recv()
-    for a in range(rows):
-        zonal(0, a, fin[0, a], unpack(lon0_in[1], lon0_in[0], a, lane))
+    zonal(0)
     send_rows(0)
     some(1)
     some(2)
@@ -564,7 +527,7 @@
         w_mid,
         b_mid.reshape(1, -1),
         w_out.T,
-        tracers.reshape(tr * lev * rows, cols),
+        tracers,
         zonal_wind,
         meridional_wind,
         mixing,
@@ -578,15 +541,14 @@
         + [
             pltpu.SMEM(mixing.shape, f32),
             pltpu.SemaphoreType.DMA((len(args),)),
-            pltpu.VMEM((2, lev + 1, 8, cols), f32),
-            pltpu.VMEM((2, lev + 1, 8, cols), f32),
-            pltpu.VMEM((2, tr, cols), f32),
-            pltpu.VMEM((2, tr, cols), f32),
+            pltpu.VMEM((lev + 1, cols + 32, tr * rows), f32),
+            pltpu.VMEM((cols + 32, tr * rows), f32),
+            pltpu.VMEM((cols, tr * rows), f32),
+            pltpu.VMEM((7 * (cols + 16), 2 * lev * rows), jnp.bfloat16),
+            pltpu.VMEM((7 * (cols + 16), tr * rows), f32),
             pltpu.VMEM((2, lev, rows, cols), f32),
             pltpu.VMEM((count, 8, cols), f32),
             pltpu.VMEM((count, 8, cols), f32),
-            pltpu.VMEM((lev, 7, rows, cols), f32),
-            pltpu.VMEM((lev, 7, rows, cols), f32),
             pltpu.VMEM((lev, 7, 3 * rows, cols), f32),
             pltpu.VMEM((lev, rows + 2 * WIDE, tr, cols), f32),
             pltpu.VMEM((lev, rows, tr, cols), f32),

time: 46.8 us -> 38.1 us (0.81)
  Pallas kernels: 44.3 us -> 35.6 us
    pallas_call x1, Pallas kernels: 44.3 us -> 35.6 us  [on_device(): pl.pallas_call(functools.partial(kernel, n_lat, n_lon, cap), out_shape=ja...]
where the time goes in v4:
time: 38.1 us; the launch traced here: 37.9 us
  Pallas kernels  35.6 us (93%)
  local copies, waits for them, and re-layouts  2.3 us (6%)
    pallas_call x1, Pallas kernels, on_device(): pl.pallas_call(functools.partial(kernel, n_lat, n_lon, cap), out_shape=ja...  35.6 us
    unnamed x1, local copies, waits for them, and re-layouts  2.3 us

profile of v4, /device:TPU:0, one launch (start us, length us, event | category | flops | bytes accessed | tf_op | source)
XLA Modules:
  0.0 37.9 jit_solution(5121729243248182340)
XLA Ops:
  0.0 35.6 %shard_map.118 = f32[2048,128]{1,0:T(8,128)} custom-call(bf16[64,512]{1,0:T(8,128)(2,1)} %bitcast.8, s32[1,512]{1,0:T(1,128)} %bitcast.10, s32[1,512]{1,0:T(1,128)} %bitcast.11, bf16[64,256]{1,0:T(8,128)(2,1)} %refs_3_.1, f32[1,256]{1,0:T(1,128)} %bitcast.12, bf16[256,256]{1,0:T(8,128)(2,1)} %refs_5_.1, f32[1,256]{1,0:T(1,128)} %bitcast.13, ...), custom_call_target="tpu_custom_call" | custom-call | tf_op jit(solution)/shard_map/pallas_call | solution.py:535
  35.6 2.3 %copy.14 = f32[16,16,8,128]{3,2,1,0:T(8,128)} copy(f32[16,16,8,128]{3,2,1,0:T(8,128)} %bitcast.7) | data formatting | bytes 2097152

commit v5 on v4

--- a/solution.py
+++ b/solution.py
@@ -82,7 +82,6 @@
     acc,
     slots,
     lon_sem,
-    lon0_sem,
     mer_sem,
     route_send,
     route_recv,
@@ -106,7 +105,6 @@
     lev, rows, _ = zon_ref.shape
     cells = feat_ref.shape[1]
     tr = st.shape[2]
-    per = lev * rows
     count = n_lat * n_lon
     groups = LANES // cap
     blocks = count // groups
@@ -167,31 +165,26 @@
     by_row = (cell % tr * rows + cell // tr == from_cell).astype(jnp.float32).astype(jnp.bfloat16)
     own = slice(16, 16 + LANES)
 
-    @pl.loop(1, lev)
-    def _(k):
-        zb[k, own] = turned_by(straight, x_ref[:, k].reshape(tr * rows, LANES))
-
+    lead = lev - 3
+
+    def turn_levels(start, stop):
+        @pl.loop(start, stop)
+        def _(k):
+            zb[k, own] = turned_by(straight, x_ref[:, k].reshape(tr * rows, LANES))
+
+    turn_levels(lead, lev)
     load(9).wait()
     zb[lev, own] = turned_by(straight, zon_ref[...].reshape(lev * rows, LANES))
 
     pl.semaphore_wait(barrier, count - 1)
 
-    def lon_copy(side):
+    def lon_copy(part, side):
+        levels = (pl.ds(lead, lev + 1 - lead), pl.ds(1, lead - 1), pl.ds(0, 1))[part]
         return pltpu.make_async_remote_copy(
-            src_ref=zb.at[pl.ds(1, lev), pl.ds((16, 8 + LANES)[side], 8)],
-            dst_ref=zb.at[pl.ds(1, lev), pl.ds((16 + LANES, 8)[side], 8)],
-            send_sem=lon_sem.at[0, side],
-            recv_sem=lon_sem.at[1, side],
-            device_id=(lat, (west, east)[side]),
-            device_id_type=MESH,
-        )
-
-    def lon0_copy(side):
-        return pltpu.make_async_remote_copy(
-            src_ref=zb.at[0, pl.ds((16, 8 + LANES)[side], 8)],
-            dst_ref=zb.at[0, pl.ds((16 + LANES, 8)[side], 8)],
-            send_sem=lon0_sem.at[0, side],
-            recv_sem=lon0_sem.at[1, side],
+            src_ref=zb.at[levels, pl.ds((16, 8 + LANES)[side], 8)],
+            dst_ref=zb.at[levels, pl.ds((16 + LANES, 8)[side], 8)],
+            send_sem=lon_sem.at[0, part, side],
+            recv_sem=lon_sem.at[1, part, side],
             device_id=(lat, (west, east)[side]),
             device_id_type=MESH,
         )
@@ -226,8 +219,8 @@
             device_id_type=MESH,
         )
 
-    lon_copy(0).start()
-    lon_copy(1).start()
+    lon_copy(0, 0).start()
+    lon_copy(0, 1).start()
     load(10).wait()
 
     @pl.when(has_south)
@@ -238,23 +231,12 @@
     def _():
         mer_copy(1).start()
 
-    for i in (0, 3, 5, 4, 6, 7, 1, 2):
-        load(i).wait()
-    first = silu(
-        lax.dot_general(
-            feat_ref[...], w_in_ref[...], (((0,), (0,)), ((), ())), preferred_element_type=jnp.float32
-        )
-        + b_in_ref[...]
-    ).astype(jnp.bfloat16)
-    second = silu(
-        jnp.dot(first, w_mid_ref[...], preferred_element_type=jnp.float32) + b_mid_ref[...]
-    ).astype(jnp.bfloat16)
-    flux = lax.dot_general(
-        w_out_ref[...], second, (((1,), (1,)), ((), ())), preferred_element_type=jnp.float32
-    )
-
-    lon_copy(0).wait_recv()
-    lon_copy(1).wait_recv()
+    turn_levels(1, lead)
+    lon_copy(1, 0).start()
+    lon_copy(1, 1).start()
+
+    lon_copy(0, 0).wait_recv()
+    lon_copy(0, 1).wait_recv()
 
     wide_cols = LANES + 16
     c = zb[lev, 8 : 8 + wide_cols]
@@ -305,10 +287,32 @@
         def _():
             lat_copy(k, 1).start()
 
-    @pl.loop(1, lev // 2)
-    def _(k):
-        zonal(k)
-        send_rows(k)
+    def blow(start, stop):
+        @pl.loop(start, stop)
+        def _(k):
+            zonal(k)
+            send_rows(k)
+
+    blow(lead, lev)
+
+    for i in (0, 3, 5, 4, 6, 7, 1, 2):
+        load(i).wait()
+    first = silu(
+        lax.dot_general(
+            feat_ref[...], w_in_ref[...], (((0,), (0,)), ((), ())), preferred_element_type=jnp.float32
+        )
+        + b_in_ref[...]
+    ).astype(jnp.bfloat16)
+    second = silu(
+        jnp.dot(first, w_mid_ref[...], preferred_element_type=jnp.float32) + b_mid_ref[...]
+    ).astype(jnp.bfloat16)
+    flux = lax.dot_general(
+        w_out_ref[...], second, (((1,), (1,)), ((), ())), preferred_element_type=jnp.float32
+    )
+
+    lon_copy(1, 0).wait_recv()
+    lon_copy(1, 1).wait_recv()
+    blow(1, lead // 2)
 
     tile = tile_ref[...]
     named = (tile == lax.broadcasted_iota(jnp.int32, (count, cells), 0)).astype(jnp.float32)
@@ -357,10 +361,7 @@
 
     route_in[place(me)] = route_out[place(me)]
 
-    @pl.loop(lev // 2, lev)
-    def _(k):
-        zonal(k)
-        send_rows(k)
+    blow(lead // 2, lead)
 
     @pl.when(has_south)
     def _():
@@ -415,8 +416,8 @@
 
     surface = x_ref[:, 0].reshape(tr * rows, LANES) + emitted
     zb[0, own] = turned_by(straight, surface)
-    lon0_copy(0).start()
-    lon0_copy(1).start()
+    lon_copy(2, 0).start()
+    lon_copy(2, 1).start()
 
     def meridional(k):
         @pl.when(has_south)
@@ -448,23 +449,36 @@
                 for j, value in zip(levels, part):
                     total = total + value * mix_ref[a, k, j]
                 if closing:
-                    out_ref[pl.ds(k * rows + a, tr, stride=per), :] = total
+                    out_ref[k, a] = total
                 else:
                     acc[a, k] = total
 
-    cuts = [1, 1 + lev // 3, 1 + 2 * (lev // 3), lev]
+    ordered = list(range(lead, lev)) + list(range(1, lead))
+    share = len(ordered) // 3
+    meet = lev - lead
 
     def some(i):
-        @pl.loop(cuts[i], cuts[i + 1])
+        levels = ordered[i * share : (i + 1) * share if i < 2 else None]
+        first = 0
+
+        if i == 0:
+
+            @pl.loop(lead, lev)
+            def _(k):
+                meridional(k)
+
+            first = meet
+
+        @pl.loop(levels[first], levels[-1] + 1)
         def _(k):
             meridional(k)
 
-        mixed(range(cuts[i], cuts[i + 1]), i == 0, False)
+        mixed(levels, i == 0, False)
 
     load(11).wait()
     some(0)
-    lon0_copy(0).wait_recv()
-    lon0_copy(1).wait_recv()
+    lon_copy(2, 0).wait_recv()
+    lon_copy(2, 1).wait_recv()
     zonal(0)
     send_rows(0)
     some(1)
@@ -473,8 +487,8 @@
     mixed(range(1), False, True)
 
     for side in range(2):
-        lon_copy(side).wait_send()
-        lon0_copy(side).wait_send()
+        for part in range(3):
+            lon_copy(part, side).wait_send()
 
     @pl.loop(1, count)
     def _(o):
@@ -534,7 +548,7 @@
     )
     out = pl.pallas_call(
         functools.partial(kernel, n_lat, n_lon, cap),
-        out_shape=jax.ShapeDtypeStruct((tr * lev * rows, cols), f32),
+        out_shape=jax.ShapeDtypeStruct((lev, rows, tr, cols), f32),
         in_specs=[pl.BlockSpec(memory_space=pltpu.HBM)] * len(args),
         out_specs=pl.BlockSpec(memory_space=pltpu.VMEM),
         scratch_shapes=[pltpu.VMEM(arg.shape, arg.dtype) for arg in args[:-1]]
@@ -554,8 +568,7 @@
             pltpu.VMEM((lev, rows, tr, cols), f32),
             pltpu.VMEM((rows, lev, tr, cols), f32),
             pltpu.VMEM((3, count * cap // cols, 8, cols), f32),
-            pltpu.SemaphoreType.DMA((2, 2)),
-            pltpu.SemaphoreType.DMA((2, 2)),
+            pltpu.SemaphoreType.DMA((2, 3, 2)),
             pltpu.SemaphoreType.DMA((2, 2)),
             pltpu.SemaphoreType.DMA((count,)),
             pltpu.SemaphoreType.DMA((count,)),
@@ -566,7 +579,7 @@
             collective_id=0, has_side_effects=True, vmem_limit_bytes=60 * 1024 * 1024
         ),
     )(*args)
-    return out.reshape(tr, lev, rows, cols)
+    return out.transpose(2, 0, 1, 3)
 
 
 def solution(mesh):

time: 38.1 us -> 36.7 us (0.963)
  Pallas kernels: 35.6 us -> 34 us
    transpose x0 -> x1, local copies, waits for them, and re-layouts: none -> 2.53 us  [on_device(): return out.transpose(2, 0, 1, 3)]
    unnamed x1 -> x0, local copies, waits for them, and re-layouts: 2.3 us -> none
    pallas_call x1, Pallas kernels: 35.6 us -> 34 us  [on_device(): pl.pallas_call(functools.partial(kernel, n_lat, n_lon, cap), out_shape=ja...]
where the time goes in v5:
time: 36.7 us; the launch traced here: 36.6 us
  Pallas kernels  34 us (93%)
  local copies, waits for them, and re-layouts  2.53 us (7%)
    pallas_call x1, Pallas kernels, on_device(): pl.pallas_call(functools.partial(kernel, n_lat, n_lon, cap), out_shape=ja...  34 us
    transpose x1, local copies, waits for them, and re-layouts, on_device(): return out.transpose(2, 0, 1, 3)  2.53 us

profile of v5, /device:TPU:0, one launch (start us, length us, event | category | flops | bytes accessed | tf_op | source)
XLA Modules:
  0.0 36.6 jit_solution(13914474762190727944)
XLA Ops:
  0.0 34.0 %shard_map.118 = f32[16,8,16,128]{3,2,1,0:T(8,128)} custom-call(bf16[64,512]{1,0:T(8,128)(2,1)} %bitcast.8, s32[1,512]{1,0:T(1,128)} %bitcast.10, s32[1,512]{1,0:T(1,128)} %bitcast.11, bf16[64,256]{1,0:T(8,128)(2,1)} %refs_3_.1, f32[1,256]{1,0:T(1,128)} %bitcast.12, bf16[256,256]{1,0:T(8,128)(2,1)} %refs_5_.1, f32[1,256]{1,0:T(1,128)} %bitcast.13, ...), custom_call_target="tpu_custom_call" | custom-call | tf_op jit(solution)/shard_map/pallas_call | solution.py:549
  34.0 2.5 %copy.13 = f32[16,16,8,128]{3,2,1,0:T(8,128)} copy(f32[16,16,8,128]{3,0,2,1:T(8,128)} %bitcast.7) | data formatting | bytes 2097152 | tf_op jit(solution)/shard_map/transpose | solution.py:582

commit v6 on v5

--- a/solution.py
+++ b/solution.py
@@ -13,7 +13,8 @@
 
 
 def silu(v):
-    return v / (1.0 + jnp.exp(-v))
+    half = 0.5 * v
+    return half + half * jnp.tanh(half)
 
 
 def face_weights(c):
@@ -87,6 +88,7 @@
     route_recv,
     lat_send,
     lat_recv,
+    out_sem,
 ):
     (
         feat_ref,
@@ -203,9 +205,29 @@
         return pltpu.make_async_remote_copy(
             src_ref=st.at[k, pl.ds((WIDE, rows)[side], WIDE)],
             dst_ref=st.at[k, pl.ds((WIDE + rows, 0)[side], WIDE)],
-            send_sem=lat_send.at[side, k],
+            send_sem=lat_send.at[side],
             recv_sem=lat_recv.at[side, k],
             device_id=(lat + (-1, 1)[side], lon),
+            device_id_type=MESH,
+        )
+
+    def lat_all(side):
+        return pltpu.make_async_remote_copy(
+            src_ref=st.at[:, pl.ds((WIDE, rows)[side], WIDE)],
+            dst_ref=st.at[:, pl.ds((WIDE + rows, 0)[side], WIDE)],
+            send_sem=lat_send.at[side],
+            recv_sem=lat_recv.at[side, 0],
+            device_id=(lat + (-1, 1)[side], lon),
+            device_id_type=MESH,
+        )
+
+    def route_all():
+        return pltpu.make_async_remote_copy(
+            src_ref=route_out.at[pl.ds(0, count - 1)],
+            dst_ref=route_in.at[pl.ds(0, count - 1)],
+            send_sem=route_send.at[0],
+            recv_sem=route_recv.at[0],
+            device_id=(lat, east),
             device_id_type=MESH,
         )
 
@@ -213,8 +235,8 @@
         return pltpu.make_async_remote_copy(
             src_ref=route_out.at[place(d)],
             dst_ref=route_in.at[place(origin)],
-            send_sem=route_send.at[d],
-            recv_sem=route_recv.at[origin],
+            send_sem=route_send.at[0],
+            recv_sem=route_recv.at[0],
             device_id=(d // n_lon, lax.rem(d, n_lon)),
             device_id_type=MESH,
         )
@@ -378,11 +400,10 @@
     def _(k):
         c = jnp.concatenate([mer_in[1, k], mer_ref[k], mer_in[0, k]], axis=0) * northern
         for m, weight in enumerate(cell_weights(c, pltpu.roll(c, 1, 0))):
-            gm[k, m] = weight
-
-    @pl.loop(1, count)
-    def _(o):
-        route_copy(me, lax.rem(me + o, count)).wait_recv()
+            gm[k, m, 0 : 3 * rows] = weight
+
+    route_all().wait_recv()
+    route_all().wait_send()
 
     lists = [jnp.zeros((8 * blocks, LANES), jnp.float32)] * 3
     for g in range(groups):
@@ -432,12 +453,12 @@
         for a in range(-3, rows + 3):
             new = 0.0
             for m in range(7):
-                new = new + st[k, a + 3 + m] * gm[k, m, a + rows : a + rows + 1]
+                new = new + st[k, a + 3 + m] * gm[k, m, pl.ds(a + rows, tr, stride=0), :]
             once.append(new)
         for a in range(rows):
             new = 0.0
             for m in range(7):
-                new = new + once[a + m] * gm[k, m, a + rows : a + rows + 1]
+                new = new + once[a + m] * gm[k, m, pl.ds(a + rows, tr, stride=0), :]
             fin[k, a] = new
 
     def mixed(levels, opening, closing):
@@ -448,10 +469,9 @@
                 total = 0.0 if opening else acc[a, k]
                 for j, value in zip(levels, part):
                     total = total + value * mix_ref[a, k, j]
-                if closing:
-                    out_ref[k, a] = total
-                else:
-                    acc[a, k] = total
+                acc[a, k] = total
+            if closing:
+                pltpu.make_async_copy(acc.at[a], out_ref.at[a], out_sem.at[a]).start()
 
     ordered = list(range(lead, lev)) + list(range(1, lead))
     share = len(ordered) // 3
@@ -486,29 +506,23 @@
     meridional(0)
     mixed(range(1), False, True)
 
+    @pl.loop(0, rows)
+    def _(a):
+        pltpu.make_async_copy(acc.at[a], out_ref.at[a], out_sem.at[a]).wait()
+
     for side in range(2):
         for part in range(3):
             lon_copy(part, side).wait_send()
 
-    @pl.loop(1, count)
-    def _(o):
-        route_copy(lax.rem(me + o, count), me).wait_send()
-
     @pl.when(has_south)
     def _():
         mer_copy(0).wait_send()
-
-        @pl.loop(0, lev)
-        def _(k):
-            lat_copy(k, 0).wait_send()
+        lat_all(0).wait_send()
 
     @pl.when(has_north)
     def _():
         mer_copy(1).wait_send()
-
-        @pl.loop(0, lev)
-        def _(k):
-            lat_copy(k, 1).wait_send()
+        lat_all(1).wait_send()
 
 
 def on_device(
@@ -548,9 +562,9 @@
     )
     out = pl.pallas_call(
         functools.partial(kernel, n_lat, n_lon, cap),
-        out_shape=jax.ShapeDtypeStruct((lev, rows, tr, cols), f32),
+        out_shape=jax.ShapeDtypeStruct((rows, lev, tr, cols), f32),
         in_specs=[pl.BlockSpec(memory_space=pltpu.HBM)] * len(args),
-        out_specs=pl.BlockSpec(memory_space=pltpu.VMEM),
+        out_specs=pl.BlockSpec(memory_space=pltpu.HBM),
         scratch_shapes=[pltpu.VMEM(arg.shape, arg.dtype) for arg in args[:-1]]
         + [
             pltpu.SMEM(mixing.shape, f32),
@@ -563,23 +577,24 @@
             pltpu.VMEM((2, lev, rows, cols), f32),
             pltpu.VMEM((count, 8, cols), f32),
             pltpu.VMEM((count, 8, cols), f32),
-            pltpu.VMEM((lev, 7, 3 * rows, cols), f32),
+            pltpu.VMEM((lev, 7, 3 * rows + tr, cols), f32),
             pltpu.VMEM((lev, rows + 2 * WIDE, tr, cols), f32),
             pltpu.VMEM((lev, rows, tr, cols), f32),
             pltpu.VMEM((rows, lev, tr, cols), f32),
             pltpu.VMEM((3, count * cap // cols, 8, cols), f32),
             pltpu.SemaphoreType.DMA((2, 3, 2)),
             pltpu.SemaphoreType.DMA((2, 2)),
-            pltpu.SemaphoreType.DMA((count,)),
-            pltpu.SemaphoreType.DMA((count,)),
+            pltpu.SemaphoreType.DMA((1,)),
+            pltpu.SemaphoreType.DMA((1,)),
+            pltpu.SemaphoreType.DMA((2,)),
             pltpu.SemaphoreType.DMA((2, lev)),
-            pltpu.SemaphoreType.DMA((2, lev)),
+            pltpu.SemaphoreType.DMA((rows,)),
         ],
         compiler_params=pltpu.CompilerParams(
             collective_id=0, has_side_effects=True, vmem_limit_bytes=60 * 1024 * 1024
         ),
     )(*args)
-    return out.transpose(2, 0, 1, 3)
+    return out.transpose(2, 1, 0, 3)
 
 
 def solution(mesh):

time: 36.7 us -> 35.7 us (0.973)
  Pallas kernels: 34 us -> 32.7 us
    pallas_call x1, Pallas kernels: 34 us -> 32.7 us  [on_device(): pl.pallas_call(functools.partial(kernel, n_lat, n_lon, cap), out_shape=ja...]
where the time goes in v6:
time: 35.7 us; the launch traced here: 35.5 us
  Pallas kernels  32.7 us (92%)
  local copies, waits for them, and re-layouts  2.81 us (8%)
    pallas_call x1, Pallas kernels, on_device(): pl.pallas_call(functools.partial(kernel, n_lat, n_lon, cap), out_shape=ja...  32.7 us
    transpose x1, local copies, waits for them, and re-layouts, on_device(): return out.transpose(2, 1, 0, 3)  2.81 us

profile of v6, /device:TPU:0, one launch (start us, length us, event | category | flops | bytes accessed | tf_op | source)
XLA Modules:
  0.0 35.5 jit_solution(2990960614236168929)
XLA Ops:
  0.0 32.7 %shard_map.118 = f32[8,16,16,128]{3,2,1,0:T(8,128)} custom-call(bf16[64,512]{1,0:T(8,128)(2,1)} %bitcast.8, s32[1,512]{1,0:T(1,128)} %bitcast.10, s32[1,512]{1,0:T(1,128)} %bitcast.11, bf16[64,256]{1,0:T(8,128)(2,1)} %refs_3_.1, f32[1,256]{1,0:T(1,128)} %bitcast.12, bf16[256,256]{1,0:T(8,128)(2,1)} %refs_5_.1, f32[1,256]{1,0:T(1,128)} %bitcast.13, ...), custom_call_target="tpu_custom_call" | custom-call | tf_op jit(solution)/shard_map/pallas_call | solution.py:563
  32.7 2.8 %copy.13 = f32[16,16,8,128]{3,2,1,0:T(8,128)} copy(f32[16,16,8,128]{3,0,1,2:T(8,128)} %bitcast.7) | data formatting | bytes 2097152 | tf_op jit(solution)/shard_map/transpose | solution.py:597

commit v7 on v6

--- a/solution.py
+++ b/solution.py
@@ -167,10 +167,10 @@
     by_row = (cell % tr * rows + cell // tr == from_cell).astype(jnp.float32).astype(jnp.bfloat16)
     own = slice(16, 16 + LANES)
 
-    lead = lev - 3
+    lead = lev - 4
 
     def turn_levels(start, stop):
-        @pl.loop(start, stop)
+        @pl.loop(start, stop, unroll=4 if (stop - start) % 4 == 0 else stop - start)
         def _(k):
             zb[k, own] = turned_by(straight, x_ref[:, k].reshape(tr * rows, LANES))
 
@@ -265,40 +265,45 @@
     before = zb[lev, 7 : 7 + wide_cols]
     for m, weight in enumerate(cell_weights(c, before)):
         wz[m * wide_cols : (m + 1) * wide_cols] = halves(weight)
-    pick_from = lax.broadcasted_iota(jnp.int32, (2 * LANES, LANES), 0) % LANES
-    pick_row = lax.broadcasted_iota(jnp.int32, (2 * LANES, LANES), 1) % rows
-
-    def zonal(k):
-        pick = (pick_from == pick_row + k * rows).astype(jnp.float32).astype(jnp.bfloat16)
+    third = wide_cols // 3
+    half = LANES // 2
+
+    def zonal(k, number):
+        lanes = [slice(j * LANES, (j + 1) * LANES) for j in range(number)]
+        shape = (2 * LANES, number * LANES)
+        pick_from = lax.broadcasted_iota(jnp.int32, shape, 0) % LANES
+        at = lax.broadcasted_iota(jnp.int32, shape, 1)
+        pick = pick_from == at % rows + (k + at // LANES) * rows
+        pick = pick.astype(jnp.float32).astype(jnp.bfloat16)
         for m in range(7):
-            wk[m * wide_cols : (m + 1) * wide_cols] = jnp.dot(
+            wk[m * wide_cols : (m + 1) * wide_cols, : number * LANES] = jnp.dot(
                 wz[m * wide_cols : (m + 1) * wide_cols], pick, preferred_element_type=jnp.float32
             )
-        third = wide_cols // 3
 
         @pl.loop(0, 3)
         def _(i):
-            new = 0.0
-            for m in range(7):
-                new = new + (
-                    zb[k, pl.ds(i * third + 5 + m, third)]
-                    * wk[pl.ds(pl.multiple_of(i * third + m * wide_cols, 8), third)]
-                )
-            once_z[pl.ds(pl.multiple_of(i * third + 8, 8), third)] = new
-
-        half = LANES // 2
+            for j in range(number):
+                new = 0.0
+                for m in range(7):
+                    new = new + (
+                        zb[k + j, pl.ds(i * third + 5 + m, third)]
+                        * wk[pl.ds(pl.multiple_of(i * third + m * wide_cols, 8), third), lanes[j]]
+                    )
+                once_z[j, pl.ds(pl.multiple_of(i * third + 8, 8), third)] = new
 
         @pl.loop(0, 2)
         def _(i):
-            new = 0.0
-            for m in range(7):
-                new = new + (
-                    once_z[pl.ds(i * half + 13 + m, half)]
-                    * wk[pl.ds(pl.multiple_of(i * half + 8 + m * wide_cols, 8), half)]
-                )
-            twice_z[pl.ds(pl.multiple_of(i * half, 8), half)] = new
-
-        st[k, WIDE : WIDE + rows] = turned_by(by_row, twice_z[...]).reshape(rows, tr, LANES)
+            for j in range(number):
+                new = 0.0
+                for m in range(7):
+                    new = new + (
+                        once_z[j, pl.ds(i * half + 13 + m, half)]
+                        * wk[pl.ds(pl.multiple_of(i * half + 8 + m * wide_cols, 8), half), lanes[j]]
+                    )
+                twice_z[j, pl.ds(pl.multiple_of(i * half, 8), half)] = new
+
+        for j in range(number):
+            st[k + j, WIDE : WIDE + rows] = turned_by(by_row, twice_z[j]).reshape(rows, tr, LANES)
 
     def send_rows(k):
         @pl.when(has_south)
@@ -310,10 +315,16 @@
             lat_copy(k, 1).start()
 
     def blow(start, stop):
-        @pl.loop(start, stop)
-        def _(k):
-            zonal(k)
+        @pl.loop(0, (stop - start) // 2)
+        def _(i):
+            k = start + 2 * i
+            zonal(k, 2)
             send_rows(k)
+            send_rows(k + 1)
+
+        if (stop - start) % 2:
+            zonal(stop - 1, 1)
+            send_rows(stop - 1)
 
     blow(lead, lev)
 
@@ -334,7 +345,7 @@
 
     lon_copy(1, 0).wait_recv()
     lon_copy(1, 1).wait_recv()
-    blow(1, lead // 2)
+    blow(1, lead // 2 + 1)
 
     tile = tile_ref[...]
     named = (tile == lax.broadcasted_iota(jnp.int32, (count, cells), 0)).astype(jnp.float32)
@@ -383,7 +394,7 @@
 
     route_in[place(me)] = route_out[place(me)]
 
-    blow(lead // 2, lead)
+    blow(lead // 2 + 1, lead)
 
     @pl.when(has_south)
     def _():
@@ -499,7 +510,7 @@
     some(0)
     lon_copy(2, 0).wait_recv()
     lon_copy(2, 1).wait_recv()
-    zonal(0)
+    zonal(0, 1)
     send_rows(0)
     some(1)
     some(2)
@@ -570,10 +581,10 @@
             pltpu.SMEM(mixing.shape, f32),
             pltpu.SemaphoreType.DMA((len(args),)),
             pltpu.VMEM((lev + 1, cols + 32, tr * rows), f32),
-            pltpu.VMEM((cols + 32, tr * rows), f32),
-            pltpu.VMEM((cols, tr * rows), f32),
+            pltpu.VMEM((2, cols + 32, tr * rows), f32),
+            pltpu.VMEM((2, cols, tr * rows), f32),
             pltpu.VMEM((7 * (cols + 16), 2 * lev * rows), jnp.bfloat16),
-            pltpu.VMEM((7 * (cols + 16), tr * rows), f32),
+            pltpu.VMEM((7 * (cols + 16), 2 * tr * rows), f32),
             pltpu.VMEM((2, lev, rows, cols), f32),
             pltpu.VMEM((count, 8, cols), f32),
             pltpu.VMEM((count, 8, cols), f32),

time: 35.7 us -> 37.7 us (1.056)
  Pallas kernels: 32.7 us -> 34.7 us
    pallas_call x1, Pallas kernels: 32.7 us -> 34.7 us  [on_device(): pl.pallas_call(functools.partial(kernel, n_lat, n_lon, cap), out_shape=ja...]
where the time goes in v7:
time: 37.7 us; the launch traced here: 37.5 us
  Pallas kernels  34.7 us (92%)
  local copies, waits for them, and re-layouts  2.81 us (7%)
    pallas_call x1, Pallas kernels, on_device(): pl.pallas_call(functools.partial(kernel, n_lat, n_lon, cap), out_shape=ja...  34.7 us
    transpose x1, local copies, waits for them, and re-layouts, on_device(): return out.transpose(2, 1, 0, 3)  2.81 us

profile of v7, /device:TPU:0, one launch (start us, length us, event | category | flops | bytes accessed | tf_op | source)
XLA Modules:
  0.0 37.5 jit_solution(13971688467497904382)
XLA Ops:
  0.0 34.7 %shard_map.118 = f32[8,16,16,128]{3,2,1,0:T(8,128)} custom-call(bf16[64,512]{1,0:T(8,128)(2,1)} %bitcast.8, s32[1,512]{1,0:T(1,128)} %bitcast.10, s32[1,512]{1,0:T(1,128)} %bitcast.11, bf16[64,256]{1,0:T(8,128)(2,1)} %refs_3_.1, f32[1,256]{1,0:T(1,128)} %bitcast.12, bf16[256,256]{1,0:T(8,128)(2,1)} %refs_5_.1, f32[1,256]{1,0:T(1,128)} %bitcast.13, ...), custom_call_target="tpu_custom_call" | custom-call | tf_op jit(solution)/shard_map/pallas_call | solution.py:574
  34.7 2.8 %copy.13 = f32[16,16,8,128]{3,2,1,0:T(8,128)} copy(f32[16,16,8,128]{3,0,1,2:T(8,128)} %bitcast.7) | data formatting | bytes 2097152 | tf_op jit(solution)/shard_map/transpose | solution.py:608
